TPU v7x, 128 devices: a whole 4x4x4 slice. The times are simulated.
128 devices in a mesh: outer: 16 (over z_hi, x, core), inner: 8 (over z_lo, y).
Axes of the slice: x: 4, y: 4, z: 4 (z_hi: 2, z_lo: 2; z = z_hi * 2 + z_lo), core: 2. Of those that a mesh axis runs over, the one named last changes fastest.
Arguments:
- queries: bfloat16 [131072, 512], P(('outer', 'inner')), may hold values from -6 to 6
- keys: bfloat16 [131072, 128], P(('outer', 'inner')), may hold values from -6 to 6
- values: bfloat16 [131072, 128], P(('outer', 'inner')), may hold values from -6 to 6
- doc_lengths: int32 [16], replicated, may hold values from 1 to 11264, 131072 in all
Outputs:
- attended: bfloat16 [131072, 512], P(('outer', 'inner'))
Inputs may be any that keep to these rules, and one draw needn't show every extreme that they name: `doc_lengths`: 16 lengths in sequence order that sum to 131072, the longest exactly 11264.
All inputs are finite; a program needn't handle non-finite values.
Results may differ from a plain program's by a relative error of at most 0.0065.
Values may be sent and summed in bfloat16 or wider, within the bound.
A program may use at most 832 MiB of HBM per device.

v0:
```python
import jax
import jax.numpy as jnp
from jax import lax
from jax.sharding import PartitionSpec as P

HEAD = 128
QHEADS = 4
REACH = 11


def from_behind(block, axis, distance):
    devices = range(lax.axis_size(axis))
    route = [(i - distance, i) for i in devices if i - distance in devices]
    return lax.ppermute(block, axis, route)


def document(positions, doc_ends):
    return jnp.sum((positions[:, None] >= doc_ends[None, :]).astype(jnp.int32), axis=1)


def attend(state_now, shaped, query_pos, query_doc, key_rows, value_rows, key_pos, doc_ends):
    top_old, total_old, summed = state_now
    key_doc = document(key_pos, doc_ends)
    visible = (query_doc[:, None] == key_doc[None, :]) & (key_pos[None, :] <= query_pos[:, None])
    visible = visible & (key_pos[None, :] >= 0)
    scores = jnp.einsum("qhd,kd->hqk", shaped, key_rows, preferred_element_type=jnp.float32)
    scores = jnp.where(visible[None], scores * HEAD ** (-0.5), -1e30)
    top_new = jnp.maximum(top_old, jnp.max(scores, axis=-1))
    weights = jnp.where(visible[None], jnp.exp(scores - top_new[..., None]), 0.0)
    factor = jnp.exp(top_old - top_new)
    total_new = total_old * factor + jnp.sum(weights, axis=-1)
    product = jnp.einsum(
        "hqk,kd->hqd", weights.astype(jnp.bfloat16), value_rows, preferred_element_type=jnp.float32
    )
    return (top_new, total_new, summed * factor[..., None] + product)


def per_device(queries, keys, values, doc_lengths):
    tok_rows = keys.shape[0]
    inner_size = lax.axis_size("inner")
    outer_index = lax.axis_index("outer")
    inner_index = lax.axis_index("inner")
    device = outer_index * inner_size + inner_index
    doc_ends = jnp.cumsum(doc_lengths)
    offsets = jnp.arange(tok_rows, dtype=jnp.int32)
    query_pos = device * tok_rows + offsets
    query_doc = document(query_pos, doc_ends)
    shaped = queries.reshape(tok_rows, QHEADS, HEAD)
    initial = (
        jnp.full((QHEADS, tok_rows), -1e30, jnp.float32),
        jnp.zeros((QHEADS, tok_rows), jnp.float32),
        jnp.zeros((QHEADS, tok_rows, HEAD), jnp.float32),
    )

    def attend_block(state_now, key_rows, value_rows, key_pos):
        return attend(
            state_now, shaped, query_pos, query_doc, key_rows, value_rows, key_pos, doc_ends
        )

    def attend_if(state_now, key_rows, value_rows, key_pos):
        return attend_block(state_now, key_rows, value_rows, key_pos)

    own_state = attend_block(initial, keys, values, query_pos)

    def turn(turn_index, loop_state):
        key_rows, value_rows, state_now = loop_state
        key_rows, value_rows = from_behind((key_rows, value_rows), ("outer", "inner"), 1)
        key_pos = (device - turn_index) * tok_rows + offsets
        return (key_rows, value_rows, attend_if(state_now, key_rows, value_rows, key_pos))

    final_loop = lax.fori_loop(1, REACH + 1, turn, (keys, values, own_state))
    final_state = final_loop[2]
    top_final, total_final, summed = final_state
    output = summed / total_final[..., None]
    return jnp.transpose(output, (1, 0, 2)).reshape(tok_rows, QHEADS * HEAD).astype(jnp.bfloat16)


def solution(mesh):
    placed = (
        P(("outer", "inner"), None),
        P(("outer", "inner"), None),
        P(("outer", "inner"), None),
        P(),
    )
    return jax.shard_map(
        per_device,
        mesh=mesh,
        in_specs=placed,
        out_specs=P(("outer", "inner"), None),
        check_vma=False,
    )
```

profile of v0, /device:TPU:64, one launch (start us, length us, event | category | flops | bytes accessed | tf_op | source)
XLA Modules:
  0.0 329.9 jit_solution(14043654908356504179)
XLA Ops:
  5.7 3.2 fusion.18
  8.9 4.2 %fusion.20 = f32[4,1024]{1,0:T(4,128)S(1)} fusion(f32[1024,1024,4]{1,0,2:T(8,128)S(1)} %get-tuple-element.286, f32[4,1024]{1,0:T(4,128)S(1)} %broadcast_maximum_fusion, pred[1024,1024]{0,1:T(8,128)(4,1)S(1)} %and_and_fusion.1), kind=kLoop, calls=%fused_computation.27 | loop fusion | flops 20967424 | bytes 17858560 | tf_op jit(solution)/shard_map/reduce_sum | solution.py:31
  13.1 6.5 %fusion.24 = f32[4,1024,128]{2,1,0:T(8,128)} fusion(f32[1024,1024,4]{1,0,2:T(8,128)S(1)} %get-tuple-element.286, f32[4,1024]{1,0:T(4,128)S(1)} %broadcast_maximum_fusion, pred[1024,1024]{0,1:T(8,128)(4,1)S(1)} %and_and_fusion.1, f32[4,1024]{1,0:T(4,128)S(1)} %get-tuple-element.283, bf16[1024,128]{1,0:T(8,128)(2,1)S(1)} %copy.50), kind=kOutput, calls=%fused_computation.32 | convolution fusion | flops 1095237632 | bytes 20217856 | tf_op jit(solution)/shard_map/hqk,kd->hqd/dot_general | solution.py:32
  20.3 306.8 %while.22 = (s32[]{:T(128)}, bf16[1024,128]{1,0:T(8,128)(2,1)S(1)}, bf16[1024,128]{1,0:T(8,128)(2,1)S(1)}, f32[4,1024]{1,0:T(4,128)S(1)}, f32[4,1024]{1,0:T(4,12...) while((s32[]{:T(128)}, bf16[1024,128]{1,0:T(8,128)(2,1)S(1)}, ...), condition=%wide.region_8.9_spmd.clone, body=%wide.region_4.0_spmd.clone.sunk | while | flops 2207312896 | bytes 80513384 | solution.py:71
  20.3 3.5 %collective-permute-start = (bf16[1024,128]{1,0:T(8,128)(2,1)S(1)}, bf16[1024,128]{1,0:T(8,128)(2,1)S(1)}, u32[]{:S(2)}, u32[]{:S(2)}) collective-permute-start(bf16[1024,128]{1,0:T(8,128)(2,1)S(1)} %get-tuple-element.380), channel_id=1, source_target_pairs={{0,1},{1,2},{2,3},{3,4},{4,5},{5,6},{6,7},{7,8},{8,9},{9,10},{10,1... | collective-permute-start | bytes 786440 | tf_op jit(solution)/shard_map/while/body/eval_jaxpr/ppermute | solution.py:14
  23.8 3.5 %collective-permute-start.1 = (bf16[1024,128]{1,0:T(8,128)(2,1)S(1)}, bf16[1024,128]{1,0:T(8,128)(2,1)S(1)}, u32[]{:S(2)}, u32[]{:S(2)}) collective-permute-start(bf16[1024,128]{1,0:T(8,128)(2,1)S(1)} %get-tuple-element.381), channel_id=1, source_target_pairs={{0,1},{1,2},{2,3},{3,4},{4,5},{5,6},{6,7},{7,8},{8,9},{9,10},{10,1... | collective-permute-start | bytes 786440 | tf_op jit(solution)/shard_map/while/body/eval_jaxpr/ppermute | solution.py:14
  28.7 3.6 %collective-permute-done = bf16[1024,128]{1,0:T(8,128)(2,1)S(1)} collective-permute-done((bf16[1024,128]{1,0:T(8,128)(2,1)S(1)}, bf16[1024,128]{1,0:T(8,128)(2,1)S(1)}, u32[]{:S(2)}, u32[]{:S(2)}) %collective-permute-start) | collective-permute-done | bytes 262176 | tf_op jit(solution)/shard_map/while/body/eval_jaxpr/ppermute | solution.py:14
  32.3 4.0 %fusion.46 = (f32[4,1024]{1,0:T(4,128)S(1)}, f32[1024,1024,4]{1,0,2:T(8,128)S(1)}) fusion(pred[1024,1024]{0,1:T(8,128)(4,1)S(1)} %and_and_fusion.3, bf16[1024,4,128]{2,0,1:T(8,128)(2,1)S(1)} %get-tuple-element.401, bf16[1024,128]{1,0:T(8,128)(2,1)S(1)} %collective-permute-done), kind=kOutput, calls=%fused_computation.4.clone.1 | convolution fusion | flops 1086320640 | bytes 19152896 | tf_op jit(solution)/shard_map/while/body/eval_jaxpr/qhd,kd->hqk/dot_general | solution.py:26
  36.4 4.2 %fusion.47 = f32[4,1024]{1,0:T(4,128)S(1)} fusion(f32[1024,1024,4]{1,0,2:T(8,128)S(1)} %get-tuple-element.363, f32[4,1024]{1,0:T(4,128)S(1)} %max.9, pred[1024,1024]{0,1:T(8,128)(4,1)S(1)} %and_and_fusion.3), kind=kLoop, calls=%fused_computation.6.clone.1 | loop fusion | flops 20967424 | bytes 17858560 | tf_op jit(solution)/shard_map/while/body/eval_jaxpr/reduce_sum | solution.py:31
  40.7 6.3 %multiply_add_fusion.5 = f32[4,1024,128]{2,1,0:T(8,128)S(1)} fusion(f32[4,1024,128]{2,1,0:T(8,128)S(1)} %copy-done, f32[1024,1024,4]{1,0,2:T(8,128)S(1)} %get-tuple-element.363, f32[4,1024]{1,0:T(4,128)S(1)} %max.9, pred[1024,1024]{0,1:T(8,128)(4,1)S(1)} %and_and_fusion.3, f32[4,1024]{1,0:T(4,128)S(1)} %get-tuple-element.365, ...), kind=kOutput, calls=%fused_computation.10.clone.1 | convolution fusion | flops 1095761920 | bytes 22315008 | tf_op jit(solution)/shard_map/while/body/eval_jaxpr/hqk,kd->hqd/dot_general | solution.py:32
  48.3 2.5 collective-permute-start
  50.9 3.5 %collective-permute-start.1 = (bf16[1024,128]{1,0:T(8,128)(2,1)S(1)}, bf16[1024,128]{1,0:T(8,128)(2,1)S(1)}, u32[]{:S(2)}, u32[]{:S(2)}) collective-permute-start(bf16[1024,128]{1,0:T(8,128)(2,1)S(1)} %get-tuple-element.381), channel_id=1, source_target_pairs={{0,1},{1,2},{2,3},{3,4},{4,5},{5,6},{6,7},{7,8},{8,9},{9,10},{10,1... | collective-permute-start | bytes 786440 | tf_op jit(solution)/shard_map/while/body/eval_jaxpr/ppermute | solution.py:14
  55.8 4.5 %collective-permute-done = bf16[1024,128]{1,0:T(8,128)(2,1)S(1)} collective-permute-done((bf16[1024,128]{1,0:T(8,128)(2,1)S(1)}, bf16[1024,128]{1,0:T(8,128)(2,1)S(1)}, u32[]{:S(2)}, u32[]{:S(2)}) %collective-permute-start) | collective-permute-done | bytes 262176 | tf_op jit(solution)/shard_map/while/body/eval_jaxpr/ppermute | solution.py:14
  60.3 4.0 %fusion.46 = (f32[4,1024]{1,0:T(4,128)S(1)}, f32[1024,1024,4]{1,0,2:T(8,128)S(1)}) fusion(pred[1024,1024]{0,1:T(8,128)(4,1)S(1)} %and_and_fusion.3, bf16[1024,4,128]{2,0,1:T(8,128)(2,1)S(1)} %get-tuple-element.401, bf16[1024,128]{1,0:T(8,128)(2,1)S(1)} %collective-permute-done), kind=kOutput, calls=%fused_computation.4.clone.1 | convolution fusion | flops 1086320640 | bytes 19152896 | tf_op jit(solution)/shard_map/while/body/eval_jaxpr/qhd,kd->hqk/dot_general | solution.py:26
  64.3 4.2 %fusion.47 = f32[4,1024]{1,0:T(4,128)S(1)} fusion(f32[1024,1024,4]{1,0,2:T(8,128)S(1)} %get-tuple-element.363, f32[4,1024]{1,0:T(4,128)S(1)} %max.9, pred[1024,1024]{0,1:T(8,128)(4,1)S(1)} %and_and_fusion.3), kind=kLoop, calls=%fused_computation.6.clone.1 | loop fusion | flops 20967424 | bytes 17858560 | tf_op jit(solution)/shard_map/while/body/eval_jaxpr/reduce_sum | solution.py:31
  68.6 6.3 %multiply_add_fusion.5 = f32[4,1024,128]{2,1,0:T(8,128)S(1)} fusion(f32[4,1024,128]{2,1,0:T(8,128)S(1)} %copy-done, f32[1024,1024,4]{1,0,2:T(8,128)S(1)} %get-tuple-element.363, f32[4,1024]{1,0:T(4,128)S(1)} %max.9, pred[1024,1024]{0,1:T(8,128)(4,1)S(1)} %and_and_fusion.3, f32[4,1024]{1,0:T(4,128)S(1)} %get-tuple-element.365, ...), kind=kOutput, calls=%fused_computation.10.clone.1 | convolution fusion | flops 1095761920 | bytes 22315008 | tf_op jit(solution)/shard_map/while/body/eval_jaxpr/hqk,kd->hqd/dot_general | solution.py:32
  76.3 1.9 collective-permute-start
  78.2 3.0 collective-permute-start.1
  82.6 5.6 %collective-permute-done = bf16[1024,128]{1,0:T(8,128)(2,1)S(1)} collective-permute-done((bf16[1024,128]{1,0:T(8,128)(2,1)S(1)}, bf16[1024,128]{1,0:T(8,128)(2,1)S(1)}, u32[]{:S(2)}, u32[]{:S(2)}) %collective-permute-start) | collective-permute-done | bytes 262176 | tf_op jit(solution)/shard_map/while/body/eval_jaxpr/ppermute | solution.py:14
  88.2 4.0 %fusion.46 = (f32[4,1024]{1,0:T(4,128)S(1)}, f32[1024,1024,4]{1,0,2:T(8,128)S(1)}) fusion(pred[1024,1024]{0,1:T(8,128)(4,1)S(1)} %and_and_fusion.3, bf16[1024,4,128]{2,0,1:T(8,128)(2,1)S(1)} %get-tuple-element.401, bf16[1024,128]{1,0:T(8,128)(2,1)S(1)} %collective-permute-done), kind=kOutput, calls=%fused_computation.4.clone.1 | convolution fusion | flops 1086320640 | bytes 19152896 | tf_op jit(solution)/shard_map/while/body/eval_jaxpr/qhd,kd->hqk/dot_general | solution.py:26
  92.2 4.2 %fusion.47 = f32[4,1024]{1,0:T(4,128)S(1)} fusion(f32[1024,1024,4]{1,0,2:T(8,128)S(1)} %get-tuple-element.363, f32[4,1024]{1,0:T(4,128)S(1)} %max.9, pred[1024,1024]{0,1:T(8,128)(4,1)S(1)} %and_and_fusion.3), kind=kLoop, calls=%fused_computation.6.clone.1 | loop fusion | flops 20967424 | bytes 17858560 | tf_op jit(solution)/shard_map/while/body/eval_jaxpr/reduce_sum | solution.py:31
  96.5 6.3 %multiply_add_fusion.5 = f32[4,1024,128]{2,1,0:T(8,128)S(1)} fusion(f32[4,1024,128]{2,1,0:T(8,128)S(1)} %copy-done, f32[1024,1024,4]{1,0,2:T(8,128)S(1)} %get-tuple-element.363, f32[4,1024]{1,0:T(4,128)S(1)} %max.9, pred[1024,1024]{0,1:T(8,128)(4,1)S(1)} %and_and_fusion.3, f32[4,1024]{1,0:T(4,128)S(1)} %get-tuple-element.365, ...), kind=kOutput, calls=%fused_computation.10.clone.1 | convolution fusion | flops 1095761920 | bytes 22315008 | tf_op jit(solution)/shard_map/while/body/eval_jaxpr/hqk,kd->hqd/dot_general | solution.py:32
  106.1 3.0 collective-permute-start.1
  110.5 5.5 %collective-permute-done = bf16[1024,128]{1,0:T(8,128)(2,1)S(1)} collective-permute-done((bf16[1024,128]{1,0:T(8,128)(2,1)S(1)}, bf16[1024,128]{1,0:T(8,128)(2,1)S(1)}, u32[]{:S(2)}, u32[]{:S(2)}) %collective-permute-start) | collective-permute-done | bytes 262176 | tf_op jit(solution)/shard_map/while/body/eval_jaxpr/ppermute | solution.py:14
  116.1 4.0 %fusion.46 = (f32[4,1024]{1,0:T(4,128)S(1)}, f32[1024,1024,4]{1,0,2:T(8,128)S(1)}) fusion(pred[1024,1024]{0,1:T(8,128)(4,1)S(1)} %and_and_fusion.3, bf16[1024,4,128]{2,0,1:T(8,128)(2,1)S(1)} %get-tuple-element.401, bf16[1024,128]{1,0:T(8,128)(2,1)S(1)} %collective-permute-done), kind=kOutput, calls=%fused_computation.4.clone.1 | convolution fusion | flops 1086320640 | bytes 19152896 | tf_op jit(solution)/shard_map/while/body/eval_jaxpr/qhd,kd->hqk/dot_general | solution.py:26
  120.1 4.2 %fusion.47 = f32[4,1024]{1,0:T(4,128)S(1)} fusion(f32[1024,1024,4]{1,0,2:T(8,128)S(1)} %get-tuple-element.363, f32[4,1024]{1,0:T(4,128)S(1)} %max.9, pred[1024,1024]{0,1:T(8,128)(4,1)S(1)} %and_and_fusion.3), kind=kLoop, calls=%fused_computation.6.clone.1 | loop fusion | flops 20967424 | bytes 17858560 | tf_op jit(solution)/shard_map/while/body/eval_jaxpr/reduce_sum | solution.py:31
  124.4 6.3 %multiply_add_fusion.5 = f32[4,1024,128]{2,1,0:T(8,128)S(1)} fusion(f32[4,1024,128]{2,1,0:T(8,128)S(1)} %copy-done, f32[1024,1024,4]{1,0,2:T(8,128)S(1)} %get-tuple-element.363, f32[4,1024]{1,0:T(4,128)S(1)} %max.9, pred[1024,1024]{0,1:T(8,128)(4,1)S(1)} %and_and_fusion.3, f32[4,1024]{1,0:T(4,128)S(1)} %get-tuple-element.365, ...), kind=kOutput, calls=%fused_computation.10.clone.1 | convolution fusion | flops 1095761920 | bytes 22315008 | tf_op jit(solution)/shard_map/while/body/eval_jaxpr/hqk,kd->hqd/dot_general | solution.py:32
  132.0 1.9 collective-permute-start
  133.9 1.9 collective-permute-start.1
  137.3 6.6 %collective-permute-done = bf16[1024,128]{1,0:T(8,128)(2,1)S(1)} collective-permute-done((bf16[1024,128]{1,0:T(8,128)(2,1)S(1)}, bf16[1024,128]{1,0:T(8,128)(2,1)S(1)}, u32[]{:S(2)}, u32[]{:S(2)}) %collective-permute-start) | collective-permute-done | bytes 262176 | tf_op jit(solution)/shard_map/while/body/eval_jaxpr/ppermute | solution.py:14
  143.9 4.0 %fusion.46 = (f32[4,1024]{1,0:T(4,128)S(1)}, f32[1024,1024,4]{1,0,2:T(8,128)S(1)}) fusion(pred[1024,1024]{0,1:T(8,128)(4,1)S(1)} %and_and_fusion.3, bf16[1024,4,128]{2,0,1:T(8,128)(2,1)S(1)} %get-tuple-element.401, bf16[1024,128]{1,0:T(8,128)(2,1)S(1)} %collective-permute-done), kind=kOutput, calls=%fused_computation.4.clone.1 | convolution fusion | flops 1086320640 | bytes 19152896 | tf_op jit(solution)/shard_map/while/body/eval_jaxpr/qhd,kd->hqk/dot_general | solution.py:26
  148.0 4.2 %fusion.47 = f32[4,1024]{1,0:T(4,128)S(1)} fusion(f32[1024,1024,4]{1,0,2:T(8,128)S(1)} %get-tuple-element.363, f32[4,1024]{1,0:T(4,128)S(1)} %max.9, pred[1024,1024]{0,1:T(8,128)(4,1)S(1)} %and_and_fusion.3), kind=kLoop, calls=%fused_computation.6.clone.1 | loop fusion | flops 20967424 | bytes 17858560 | tf_op jit(solution)/shard_map/while/body/eval_jaxpr/reduce_sum | solution.py:31
  152.3 6.3 %multiply_add_fusion.5 = f32[4,1024,128]{2,1,0:T(8,128)S(1)} fusion(f32[4,1024,128]{2,1,0:T(8,128)S(1)} %copy-done, f32[1024,1024,4]{1,0,2:T(8,128)S(1)} %get-tuple-element.363, f32[4,1024]{1,0:T(4,128)S(1)} %max.9, pred[1024,1024]{0,1:T(8,128)(4,1)S(1)} %and_and_fusion.3, f32[4,1024]{1,0:T(4,128)S(1)} %get-tuple-element.365, ...), kind=kOutput, calls=%fused_computation.10.clone.1 | convolution fusion | flops 1095761920 | bytes 22315008 | tf_op jit(solution)/shard_map/while/body/eval_jaxpr/hqk,kd->hqd/dot_general | solution.py:32
  161.8 1.9 collective-permute-start.1
  165.2 6.6 %collective-permute-done = bf16[1024,128]{1,0:T(8,128)(2,1)S(1)} collective-permute-done((bf16[1024,128]{1,0:T(8,128)(2,1)S(1)}, bf16[1024,128]{1,0:T(8,128)(2,1)S(1)}, u32[]{:S(2)}, u32[]{:S(2)}) %collective-permute-start) | collective-permute-done | bytes 262176 | tf_op jit(solution)/shard_map/while/body/eval_jaxpr/ppermute | solution.py:14
  171.8 4.0 %fusion.46 = (f32[4,1024]{1,0:T(4,128)S(1)}, f32[1024,1024,4]{1,0,2:T(8,128)S(1)}) fusion(pred[1024,1024]{0,1:T(8,128)(4,1)S(1)} %and_and_fusion.3, bf16[1024,4,128]{2,0,1:T(8,128)(2,1)S(1)} %get-tuple-element.401, bf16[1024,128]{1,0:T(8,128)(2,1)S(1)} %collective-permute-done), kind=kOutput, calls=%fused_computation.4.clone.1 | convolution fusion | flops 1086320640 | bytes 19152896 | tf_op jit(solution)/shard_map/while/body/eval_jaxpr/qhd,kd->hqk/dot_general | solution.py:26
  175.8 4.2 %fusion.47 = f32[4,1024]{1,0:T(4,128)S(1)} fusion(f32[1024,1024,4]{1,0,2:T(8,128)S(1)} %get-tuple-element.363, f32[4,1024]{1,0:T(4,128)S(1)} %max.9, pred[1024,1024]{0,1:T(8,128)(4,1)S(1)} %and_and_fusion.3), kind=kLoop, calls=%fused_computation.6.clone.1 | loop fusion | flops 20967424 | bytes 17858560 | tf_op jit(solution)/shard_map/while/body/eval_jaxpr/reduce_sum | solution.py:31
  180.1 6.3 %multiply_add_fusion.5 = f32[4,1024,128]{2,1,0:T(8,128)S(1)} fusion(f32[4,1024,128]{2,1,0:T(8,128)S(1)} %copy-done, f32[1024,1024,4]{1,0,2:T(8,128)S(1)} %get-tuple-element.363, f32[4,1024]{1,0:T(4,128)S(1)} %max.9, pred[1024,1024]{0,1:T(8,128)(4,1)S(1)} %and_and_fusion.3, f32[4,1024]{1,0:T(4,128)S(1)} %get-tuple-element.365, ...), kind=kOutput, calls=%fused_computation.10.clone.1 | convolution fusion | flops 1095761920 | bytes 22315008 | tf_op jit(solution)/shard_map/while/body/eval_jaxpr/hqk,kd->hqd/dot_general | solution.py:32
  189.7 1.9 collective-permute-start.1
  193.0 6.6 %collective-permute-done = bf16[1024,128]{1,0:T(8,128)(2,1)S(1)} collective-permute-done((bf16[1024,128]{1,0:T(8,128)(2,1)S(1)}, bf16[1024,128]{1,0:T(8,128)(2,1)S(1)}, u32[]{:S(2)}, u32[]{:S(2)}) %collective-permute-start) | collective-permute-done | bytes 262176 | tf_op jit(solution)/shard_map/while/body/eval_jaxpr/ppermute | solution.py:14
  199.7 4.0 %fusion.46 = (f32[4,1024]{1,0:T(4,128)S(1)}, f32[1024,1024,4]{1,0,2:T(8,128)S(1)}) fusion(pred[1024,1024]{0,1:T(8,128)(4,1)S(1)} %and_and_fusion.3, bf16[1024,4,128]{2,0,1:T(8,128)(2,1)S(1)} %get-tuple-element.401, bf16[1024,128]{1,0:T(8,128)(2,1)S(1)} %collective-permute-done), kind=kOutput, calls=%fused_computation.4.clone.1 | convolution fusion | flops 1086320640 | bytes 19152896 | tf_op jit(solution)/shard_map/while/body/eval_jaxpr/qhd,kd->hqk/dot_general | solution.py:26
  203.7 4.2 %fusion.47 = f32[4,1024]{1,0:T(4,128)S(1)} fusion(f32[1024,1024,4]{1,0,2:T(8,128)S(1)} %get-tuple-element.363, f32[4,1024]{1,0:T(4,128)S(1)} %max.9, pred[1024,1024]{0,1:T(8,128)(4,1)S(1)} %and_and_fusion.3), kind=kLoop, calls=%fused_computation.6.clone.1 | loop fusion | flops 20967424 | bytes 17858560 | tf_op jit(solution)/shard_map/while/body/eval_jaxpr/reduce_sum | solution.py:31
  208.0 6.3 %multiply_add_fusion.5 = f32[4,1024,128]{2,1,0:T(8,128)S(1)} fusion(f32[4,1024,128]{2,1,0:T(8,128)S(1)} %copy-done, f32[1024,1024,4]{1,0,2:T(8,128)S(1)} %get-tuple-element.363, f32[4,1024]{1,0:T(4,128)S(1)} %max.9, pred[1024,1024]{0,1:T(8,128)(4,1)S(1)} %and_and_fusion.3, f32[4,1024]{1,0:T(4,128)S(1)} %get-tuple-element.365, ...), kind=kOutput, calls=%fused_computation.10.clone.1 | convolution fusion | flops 1095761920 | bytes 22315008 | tf_op jit(solution)/shard_map/while/body/eval_jaxpr/hqk,kd->hqd/dot_general | solution.py:32
  217.6 1.9 collective-permute-start.1
  220.9 6.6 %collective-permute-done = bf16[1024,128]{1,0:T(8,128)(2,1)S(1)} collective-permute-done((bf16[1024,128]{1,0:T(8,128)(2,1)S(1)}, bf16[1024,128]{1,0:T(8,128)(2,1)S(1)}, u32[]{:S(2)}, u32[]{:S(2)}) %collective-permute-start) | collective-permute-done | bytes 262176 | tf_op jit(solution)/shard_map/while/body/eval_jaxpr/ppermute | solution.py:14
  227.5 4.0 %fusion.46 = (f32[4,1024]{1,0:T(4,128)S(1)}, f32[1024,1024,4]{1,0,2:T(8,128)S(1)}) fusion(pred[1024,1024]{0,1:T(8,128)(4,1)S(1)} %and_and_fusion.3, bf16[1024,4,128]{2,0,1:T(8,128)(2,1)S(1)} %get-tuple-element.401, bf16[1024,128]{1,0:T(8,128)(2,1)S(1)} %collective-permute-done), kind=kOutput, calls=%fused_computation.4.clone.1 | convolution fusion | flops 1086320640 | bytes 19152896 | tf_op jit(solution)/shard_map/while/body/eval_jaxpr/qhd,kd->hqk/dot_general | solution.py:26
  231.6 4.2 %fusion.47 = f32[4,1024]{1,0:T(4,128)S(1)} fusion(f32[1024,1024,4]{1,0,2:T(8,128)S(1)} %get-tuple-element.363, f32[4,1024]{1,0:T(4,128)S(1)} %max.9, pred[1024,1024]{0,1:T(8,128)(4,1)S(1)} %and_and_fusion.3), kind=kLoop, calls=%fused_computation.6.clone.1 | loop fusion | flops 20967424 | bytes 17858560 | tf_op jit(solution)/shard_map/while/body/eval_jaxpr/reduce_sum | solution.py:31
  235.9 6.3 %multiply_add_fusion.5 = f32[4,1024,128]{2,1,0:T(8,128)S(1)} fusion(f32[4,1024,128]{2,1,0:T(8,128)S(1)} %copy-done, f32[1024,1024,4]{1,0,2:T(8,128)S(1)} %get-tuple-element.363, f32[4,1024]{1,0:T(4,128)S(1)} %max.9, pred[1024,1024]{0,1:T(8,128)(4,1)S(1)} %and_and_fusion.3, f32[4,1024]{1,0:T(4,128)S(1)} %get-tuple-element.365, ...), kind=kOutput, calls=%fused_computation.10.clone.1 | convolution fusion | flops 1095761920 | bytes 22315008 | tf_op jit(solution)/shard_map/while/body/eval_jaxpr/hqk,kd->hqd/dot_general | solution.py:32
  245.4 1.9 collective-permute-start.1
  248.8 6.6 %collective-permute-done = bf16[1024,128]{1,0:T(8,128)(2,1)S(1)} collective-permute-done((bf16[1024,128]{1,0:T(8,128)(2,1)S(1)}, bf16[1024,128]{1,0:T(8,128)(2,1)S(1)}, u32[]{:S(2)}, u32[]{:S(2)}) %collective-permute-start) | collective-permute-done | bytes 262176 | tf_op jit(solution)/shard_map/while/body/eval_jaxpr/ppermute | solution.py:14
  255.4 4.0 %fusion.46 = (f32[4,1024]{1,0:T(4,128)S(1)}, f32[1024,1024,4]{1,0,2:T(8,128)S(1)}) fusion(pred[1024,1024]{0,1:T(8,128)(4,1)S(1)} %and_and_fusion.3, bf16[1024,4,128]{2,0,1:T(8,128)(2,1)S(1)} %get-tuple-element.401, bf16[1024,128]{1,0:T(8,128)(2,1)S(1)} %collective-permute-done), kind=kOutput, calls=%fused_computation.4.clone.1 | convolution fusion | flops 1086320640 | bytes 19152896 | tf_op jit(solution)/shard_map/while/body/eval_jaxpr/qhd,kd->hqk/dot_general | solution.py:26
  259.5 4.2 %fusion.47 = f32[4,1024]{1,0:T(4,128)S(1)} fusion(f32[1024,1024,4]{1,0,2:T(8,128)S(1)} %get-tuple-element.363, f32[4,1024]{1,0:T(4,128)S(1)} %max.9, pred[1024,1024]{0,1:T(8,128)(4,1)S(1)} %and_and_fusion.3), kind=kLoop, calls=%fused_computation.6.clone.1 | loop fusion | flops 20967424 | bytes 17858560 | tf_op jit(solution)/shard_map/while/body/eval_jaxpr/reduce_sum | solution.py:31
  263.8 6.3 %multiply_add_fusion.5 = f32[4,1024,128]{2,1,0:T(8,128)S(1)} fusion(f32[4,1024,128]{2,1,0:T(8,128)S(1)} %copy-done, f32[1024,1024,4]{1,0,2:T(8,128)S(1)} %get-tuple-element.363, f32[4,1024]{1,0:T(4,128)S(1)} %max.9, pred[1024,1024]{0,1:T(8,128)(4,1)S(1)} %and_and_fusion.3, f32[4,1024]{1,0:T(4,128)S(1)} %get-tuple-element.365, ...), kind=kOutput, calls=%fused_computation.10.clone.1 | convolution fusion | flops 1095761920 | bytes 22315008 | tf_op jit(solution)/shard_map/while/body/eval_jaxpr/hqk,kd->hqd/dot_general | solution.py:32
  273.3 1.9 collective-permute-start.1
  276.7 6.6 %collective-permute-done = bf16[1024,128]{1,0:T(8,128)(2,1)S(1)} collective-permute-done((bf16[1024,128]{1,0:T(8,128)(2,1)S(1)}, bf16[1024,128]{1,0:T(8,128)(2,1)S(1)}, u32[]{:S(2)}, u32[]{:S(2)}) %collective-permute-start) | collective-permute-done | bytes 262176 | tf_op jit(solution)/shard_map/while/body/eval_jaxpr/ppermute | solution.py:14
  283.3 4.0 %fusion.46 = (f32[4,1024]{1,0:T(4,128)S(1)}, f32[1024,1024,4]{1,0,2:T(8,128)S(1)}) fusion(pred[1024,1024]{0,1:T(8,128)(4,1)S(1)} %and_and_fusion.3, bf16[1024,4,128]{2,0,1:T(8,128)(2,1)S(1)} %get-tuple-element.401, bf16[1024,128]{1,0:T(8,128)(2,1)S(1)} %collective-permute-done), kind=kOutput, calls=%fused_computation.4.clone.1 | convolution fusion | flops 1086320640 | bytes 19152896 | tf_op jit(solution)/shard_map/while/body/eval_jaxpr/qhd,kd->hqk/dot_general | solution.py:26
  287.3 4.2 %fusion.47 = f32[4,1024]{1,0:T(4,128)S(1)} fusion(f32[1024,1024,4]{1,0,2:T(8,128)S(1)} %get-tuple-element.363, f32[4,1024]{1,0:T(4,128)S(1)} %max.9, pred[1024,1024]{0,1:T(8,128)(4,1)S(1)} %and_and_fusion.3), kind=kLoop, calls=%fused_computation.6.clone.1 | loop fusion | flops 20967424 | bytes 17858560 | tf_op jit(solution)/shard_map/while/body/eval_jaxpr/reduce_sum | solution.py:31
  291.6 6.3 %multiply_add_fusion.5 = f32[4,1024,128]{2,1,0:T(8,128)S(1)} fusion(f32[4,1024,128]{2,1,0:T(8,128)S(1)} %copy-done, f32[1024,1024,4]{1,0,2:T(8,128)S(1)} %get-tuple-element.363, f32[4,1024]{1,0:T(4,128)S(1)} %max.9, pred[1024,1024]{0,1:T(8,128)(4,1)S(1)} %and_and_fusion.3, f32[4,1024]{1,0:T(4,128)S(1)} %get-tuple-element.365, ...), kind=kOutput, calls=%fused_computation.10.clone.1 | convolution fusion | flops 1095761920 | bytes 22315008 | tf_op jit(solution)/shard_map/while/body/eval_jaxpr/hqk,kd->hqd/dot_general | solution.py:32
  301.2 1.9 collective-permute-start.1
  304.5 6.6 %collective-permute-done = bf16[1024,128]{1,0:T(8,128)(2,1)S(1)} collective-permute-done((bf16[1024,128]{1,0:T(8,128)(2,1)S(1)}, bf16[1024,128]{1,0:T(8,128)(2,1)S(1)}, u32[]{:S(2)}, u32[]{:S(2)}) %collective-permute-start) | collective-permute-done | bytes 262176 | tf_op jit(solution)/shard_map/while/body/eval_jaxpr/ppermute | solution.py:14
  311.2 4.0 %fusion.46 = (f32[4,1024]{1,0:T(4,128)S(1)}, f32[1024,1024,4]{1,0,2:T(8,128)S(1)}) fusion(pred[1024,1024]{0,1:T(8,128)(4,1)S(1)} %and_and_fusion.3, bf16[1024,4,128]{2,0,1:T(8,128)(2,1)S(1)} %get-tuple-element.401, bf16[1024,128]{1,0:T(8,128)(2,1)S(1)} %collective-permute-done), kind=kOutput, calls=%fused_computation.4.clone.1 | convolution fusion | flops 1086320640 | bytes 19152896 | tf_op jit(solution)/shard_map/while/body/eval_jaxpr/qhd,kd->hqk/dot_general | solution.py:26
  315.2 4.2 %fusion.47 = f32[4,1024]{1,0:T(4,128)S(1)} fusion(f32[1024,1024,4]{1,0,2:T(8,128)S(1)} %get-tuple-element.363, f32[4,1024]{1,0:T(4,128)S(1)} %max.9, pred[1024,1024]{0,1:T(8,128)(4,1)S(1)} %and_and_fusion.3), kind=kLoop, calls=%fused_computation.6.clone.1 | loop fusion | flops 20967424 | bytes 17858560 | tf_op jit(solution)/shard_map/while/body/eval_jaxpr/reduce_sum | solution.py:31
  319.5 6.3 %multiply_add_fusion.5 = f32[4,1024,128]{2,1,0:T(8,128)S(1)} fusion(f32[4,1024,128]{2,1,0:T(8,128)S(1)} %copy-done, f32[1024,1024,4]{1,0,2:T(8,128)S(1)} %get-tuple-element.363, f32[4,1024]{1,0:T(4,128)S(1)} %max.9, pred[1024,1024]{0,1:T(8,128)(4,1)S(1)} %and_and_fusion.3, f32[4,1024]{1,0:T(4,128)S(1)} %get-tuple-element.365, ...), kind=kOutput, calls=%fused_computation.10.clone.1 | convolution fusion | flops 1095761920 | bytes 22315008 | tf_op jit(solution)/shard_map/while/body/eval_jaxpr/hqk,kd->hqd/dot_general | solution.py:32
  327.1 2.7 copy_bitcast_fusion
  (174 shorter events, 50.7 us)
Async XLA Ops:
  20.3 12.0 %collective-permute-start = (bf16[1024,128]{1,0:T(8,128)(2,1)S(1)}, bf16[1024,128]{1,0:T(8,128)(2,1)S(1)}, u32[]{:S(2)}, u32[]{:S(2)}) collective-permute-start(bf16[1024,128]{1,0:T(8,128)(2,1)S(1)} %get-tuple-element.380), channel_id=1, source_target_pairs={{0,1},{1,2},{2,3},{3,4},{4,5},{5,6},{6,7},{7,8},{8,9},{9,10},{10,1... | collective-permute-start | bytes 786440 | tf_op jit(solution)/shard_map/while/body/eval_jaxpr/ppermute | solution.py:14
  23.8 16.8 %collective-permute-start.1 = (bf16[1024,128]{1,0:T(8,128)(2,1)S(1)}, bf16[1024,128]{1,0:T(8,128)(2,1)S(1)}, u32[]{:S(2)}, u32[]{:S(2)}) collective-permute-start(bf16[1024,128]{1,0:T(8,128)(2,1)S(1)} %get-tuple-element.381), channel_id=1, source_target_pairs={{0,1},{1,2},{2,3},{3,4},{4,5},{5,6},{6,7},{7,8},{8,9},{9,10},{10,1... | collective-permute-start | bytes 786440 | tf_op jit(solution)/shard_map/while/body/eval_jaxpr/ppermute | solution.py:14
  36.3 4.3 %copy-start = (f32[4,1024,128]{2,1,0:T(8,128)S(1)}, f32[4,1024,128]{2,1,0:T(8,128)}, u32[]{:S(2)}) copy-start(f32[4,1024,128]{2,1,0:T(8,128)} %get-tuple-element.384) | copy-start | bytes 6291460 | tf_op jit(solution)/shard_map/while
  47.0 1.4 copy-start.1
  48.3 12.0 %collective-permute-start = (bf16[1024,128]{1,0:T(8,128)(2,1)S(1)}, bf16[1024,128]{1,0:T(8,128)(2,1)S(1)}, u32[]{:S(2)}, u32[]{:S(2)}) collective-permute-start(bf16[1024,128]{1,0:T(8,128)(2,1)S(1)} %get-tuple-element.380), channel_id=1, source_target_pairs={{0,1},{1,2},{2,3},{3,4},{4,5},{5,6},{6,7},{7,8},{8,9},{9,10},{10,1... | collective-permute-start | bytes 786440 | tf_op jit(solution)/shard_map/while/body/eval_jaxpr/ppermute | solution.py:14
  50.9 17.7 %collective-permute-start.1 = (bf16[1024,128]{1,0:T(8,128)(2,1)S(1)}, bf16[1024,128]{1,0:T(8,128)(2,1)S(1)}, u32[]{:S(2)}, u32[]{:S(2)}) collective-permute-start(bf16[1024,128]{1,0:T(8,128)(2,1)S(1)} %get-tuple-element.381), channel_id=1, source_target_pairs={{0,1},{1,2},{2,3},{3,4},{4,5},{5,6},{6,7},{7,8},{8,9},{9,10},{10,1... | collective-permute-start | bytes 786440 | tf_op jit(solution)/shard_map/while/body/eval_jaxpr/ppermute | solution.py:14
  64.3 4.3 %copy-start = (f32[4,1024,128]{2,1,0:T(8,128)S(1)}, f32[4,1024,128]{2,1,0:T(8,128)}, u32[]{:S(2)}) copy-start(f32[4,1024,128]{2,1,0:T(8,128)} %get-tuple-element.384) | copy-start | bytes 6291460 | tf_op jit(solution)/shard_map/while
  74.9 1.4 copy-start.1
  76.3 11.9 %collective-permute-start = (bf16[1024,128]{1,0:T(8,128)(2,1)S(1)}, bf16[1024,128]{1,0:T(8,128)(2,1)S(1)}, u32[]{:S(2)}, u32[]{:S(2)}) collective-permute-start(bf16[1024,128]{1,0:T(8,128)(2,1)S(1)} %get-tuple-element.380), channel_id=1, source_target_pairs={{0,1},{1,2},{2,3},{3,4},{4,5},{5,6},{6,7},{7,8},{8,9},{9,10},{10,1... | collective-permute-start | bytes 786440 | tf_op jit(solution)/shard_map/while/body/eval_jaxpr/ppermute | solution.py:14
  78.2 18.3 %collective-permute-start.1 = (bf16[1024,128]{1,0:T(8,128)(2,1)S(1)}, bf16[1024,128]{1,0:T(8,128)(2,1)S(1)}, u32[]{:S(2)}, u32[]{:S(2)}) collective-permute-start(bf16[1024,128]{1,0:T(8,128)(2,1)S(1)} %get-tuple-element.381), channel_id=1, source_target_pairs={{0,1},{1,2},{2,3},{3,4},{4,5},{5,6},{6,7},{7,8},{8,9},{9,10},{10,1... | collective-permute-start | bytes 786440 | tf_op jit(solution)/shard_map/while/body/eval_jaxpr/ppermute | solution.py:14
  92.2 4.3 %copy-start = (f32[4,1024,128]{2,1,0:T(8,128)S(1)}, f32[4,1024,128]{2,1,0:T(8,128)}, u32[]{:S(2)}) copy-start(f32[4,1024,128]{2,1,0:T(8,128)} %get-tuple-element.384) | copy-start | bytes 6291460 | tf_op jit(solution)/shard_map/while
  102.8 1.4 copy-start.1
  104.2 11.9 %collective-permute-start = (bf16[1024,128]{1,0:T(8,128)(2,1)S(1)}, bf16[1024,128]{1,0:T(8,128)(2,1)S(1)}, u32[]{:S(2)}, u32[]{:S(2)}) collective-permute-start(bf16[1024,128]{1,0:T(8,128)(2,1)S(1)} %get-tuple-element.380), channel_id=1, source_target_pairs={{0,1},{1,2},{2,3},{3,4},{4,5},{5,6},{6,7},{7,8},{8,9},{9,10},{10,1... | collective-permute-start | bytes 786440 | tf_op jit(solution)/shard_map/while/body/eval_jaxpr/ppermute | solution.py:14
  106.1 18.3 %collective-permute-start.1 = (bf16[1024,128]{1,0:T(8,128)(2,1)S(1)}, bf16[1024,128]{1,0:T(8,128)(2,1)S(1)}, u32[]{:S(2)}, u32[]{:S(2)}) collective-permute-start(bf16[1024,128]{1,0:T(8,128)(2,1)S(1)} %get-tuple-element.381), channel_id=1, source_target_pairs={{0,1},{1,2},{2,3},{3,4},{4,5},{5,6},{6,7},{7,8},{8,9},{9,10},{10,1... | collective-permute-start | bytes 786440 | tf_op jit(solution)/shard_map/while/body/eval_jaxpr/ppermute | solution.py:14
  120.1 4.3 %copy-start = (f32[4,1024,128]{2,1,0:T(8,128)S(1)}, f32[4,1024,128]{2,1,0:T(8,128)}, u32[]{:S(2)}) copy-start(f32[4,1024,128]{2,1,0:T(8,128)} %get-tuple-element.384) | copy-start | bytes 6291460 | tf_op jit(solution)/shard_map/while
  130.7 1.4 copy-start.1
  132.0 11.9 %collective-permute-start = (bf16[1024,128]{1,0:T(8,128)(2,1)S(1)}, bf16[1024,128]{1,0:T(8,128)(2,1)S(1)}, u32[]{:S(2)}, u32[]{:S(2)}) collective-permute-start(bf16[1024,128]{1,0:T(8,128)(2,1)S(1)} %get-tuple-element.380), channel_id=1, source_target_pairs={{0,1},{1,2},{2,3},{3,4},{4,5},{5,6},{6,7},{7,8},{8,9},{9,10},{10,1... | collective-permute-start | bytes 786440 | tf_op jit(solution)/shard_map/while/body/eval_jaxpr/ppermute | solution.py:14
  133.9 18.3 %collective-permute-start.1 = (bf16[1024,128]{1,0:T(8,128)(2,1)S(1)}, bf16[1024,128]{1,0:T(8,128)(2,1)S(1)}, u32[]{:S(2)}, u32[]{:S(2)}) collective-permute-start(bf16[1024,128]{1,0:T(8,128)(2,1)S(1)} %get-tuple-element.381), channel_id=1, source_target_pairs={{0,1},{1,2},{2,3},{3,4},{4,5},{5,6},{6,7},{7,8},{8,9},{9,10},{10,1... | collective-permute-start | bytes 786440 | tf_op jit(solution)/shard_map/while/body/eval_jaxpr/ppermute | solution.py:14
  147.9 4.3 %copy-start = (f32[4,1024,128]{2,1,0:T(8,128)S(1)}, f32[4,1024,128]{2,1,0:T(8,128)}, u32[]{:S(2)}) copy-start(f32[4,1024,128]{2,1,0:T(8,128)} %get-tuple-element.384) | copy-start | bytes 6291460 | tf_op jit(solution)/shard_map/while
  158.5 1.4 copy-start.1
  159.9 11.9 %collective-permute-start = (bf16[1024,128]{1,0:T(8,128)(2,1)S(1)}, bf16[1024,128]{1,0:T(8,128)(2,1)S(1)}, u32[]{:S(2)}, u32[]{:S(2)}) collective-permute-start(bf16[1024,128]{1,0:T(8,128)(2,1)S(1)} %get-tuple-element.380), channel_id=1, source_target_pairs={{0,1},{1,2},{2,3},{3,4},{4,5},{5,6},{6,7},{7,8},{8,9},{9,10},{10,1... | collective-permute-start | bytes 786440 | tf_op jit(solution)/shard_map/while/body/eval_jaxpr/ppermute | solution.py:14
  161.8 18.3 %collective-permute-start.1 = (bf16[1024,128]{1,0:T(8,128)(2,1)S(1)}, bf16[1024,128]{1,0:T(8,128)(2,1)S(1)}, u32[]{:S(2)}, u32[]{:S(2)}) collective-permute-start(bf16[1024,128]{1,0:T(8,128)(2,1)S(1)} %get-tuple-element.381), channel_id=1, source_target_pairs={{0,1},{1,2},{2,3},{3,4},{4,5},{5,6},{6,7},{7,8},{8,9},{9,10},{10,1... | collective-permute-start | bytes 786440 | tf_op jit(solution)/shard_map/while/body/eval_jaxpr/ppermute | solution.py:14
  175.8 4.3 %copy-start = (f32[4,1024,128]{2,1,0:T(8,128)S(1)}, f32[4,1024,128]{2,1,0:T(8,128)}, u32[]{:S(2)}) copy-start(f32[4,1024,128]{2,1,0:T(8,128)} %get-tuple-element.384) | copy-start | bytes 6291460 | tf_op jit(solution)/shard_map/while
  186.4 1.4 copy-start.1
  187.8 11.9 %collective-permute-start = (bf16[1024,128]{1,0:T(8,128)(2,1)S(1)}, bf16[1024,128]{1,0:T(8,128)(2,1)S(1)}, u32[]{:S(2)}, u32[]{:S(2)}) collective-permute-start(bf16[1024,128]{1,0:T(8,128)(2,1)S(1)} %get-tuple-element.380), channel_id=1, source_target_pairs={{0,1},{1,2},{2,3},{3,4},{4,5},{5,6},{6,7},{7,8},{8,9},{9,10},{10,1... | collective-permute-start | bytes 786440 | tf_op jit(solution)/shard_map/while/body/eval_jaxpr/ppermute | solution.py:14
  189.7 18.3 %collective-permute-start.1 = (bf16[1024,128]{1,0:T(8,128)(2,1)S(1)}, bf16[1024,128]{1,0:T(8,128)(2,1)S(1)}, u32[]{:S(2)}, u32[]{:S(2)}) collective-permute-start(bf16[1024,128]{1,0:T(8,128)(2,1)S(1)} %get-tuple-element.381), channel_id=1, source_target_pairs={{0,1},{1,2},{2,3},{3,4},{4,5},{5,6},{6,7},{7,8},{8,9},{9,10},{10,1... | collective-permute-start | bytes 786440 | tf_op jit(solution)/shard_map/while/body/eval_jaxpr/ppermute | solution.py:14
  203.7 4.3 %copy-start = (f32[4,1024,128]{2,1,0:T(8,128)S(1)}, f32[4,1024,128]{2,1,0:T(8,128)}, u32[]{:S(2)}) copy-start(f32[4,1024,128]{2,1,0:T(8,128)} %get-tuple-element.384) | copy-start | bytes 6291460 | tf_op jit(solution)/shard_map/while
  214.3 1.4 copy-start.1
  215.6 11.9 %collective-permute-start = (bf16[1024,128]{1,0:T(8,128)(2,1)S(1)}, bf16[1024,128]{1,0:T(8,128)(2,1)S(1)}, u32[]{:S(2)}, u32[]{:S(2)}) collective-permute-start(bf16[1024,128]{1,0:T(8,128)(2,1)S(1)} %get-tuple-element.380), channel_id=1, source_target_pairs={{0,1},{1,2},{2,3},{3,4},{4,5},{5,6},{6,7},{7,8},{8,9},{9,10},{10,1... | collective-permute-start | bytes 786440 | tf_op jit(solution)/shard_map/while/body/eval_jaxpr/ppermute | solution.py:14
  217.6 18.3 %collective-permute-start.1 = (bf16[1024,128]{1,0:T(8,128)(2,1)S(1)}, bf16[1024,128]{1,0:T(8,128)(2,1)S(1)}, u32[]{:S(2)}, u32[]{:S(2)}) collective-permute-start(bf16[1024,128]{1,0:T(8,128)(2,1)S(1)} %get-tuple-element.381), channel_id=1, source_target_pairs={{0,1},{1,2},{2,3},{3,4},{4,5},{5,6},{6,7},{7,8},{8,9},{9,10},{10,1... | collective-permute-start | bytes 786440 | tf_op jit(solution)/shard_map/while/body/eval_jaxpr/ppermute | solution.py:14
  231.6 4.3 %copy-start = (f32[4,1024,128]{2,1,0:T(8,128)S(1)}, f32[4,1024,128]{2,1,0:T(8,128)}, u32[]{:S(2)}) copy-start(f32[4,1024,128]{2,1,0:T(8,128)} %get-tuple-element.384) | copy-start | bytes 6291460 | tf_op jit(solution)/shard_map/while
  242.2 1.4 copy-start.1
  243.5 11.9 %collective-permute-start = (bf16[1024,128]{1,0:T(8,128)(2,1)S(1)}, bf16[1024,128]{1,0:T(8,128)(2,1)S(1)}, u32[]{:S(2)}, u32[]{:S(2)}) collective-permute-start(bf16[1024,128]{1,0:T(8,128)(2,1)S(1)} %get-tuple-element.380), channel_id=1, source_target_pairs={{0,1},{1,2},{2,3},{3,4},{4,5},{5,6},{6,7},{7,8},{8,9},{9,10},{10,1... | collective-permute-start | bytes 786440 | tf_op jit(solution)/shard_map/while/body/eval_jaxpr/ppermute | solution.py:14
  245.4 18.3 %collective-permute-start.1 = (bf16[1024,128]{1,0:T(8,128)(2,1)S(1)}, bf16[1024,128]{1,0:T(8,128)(2,1)S(1)}, u32[]{:S(2)}, u32[]{:S(2)}) collective-permute-start(bf16[1024,128]{1,0:T(8,128)(2,1)S(1)} %get-tuple-element.381), channel_id=1, source_target_pairs={{0,1},{1,2},{2,3},{3,4},{4,5},{5,6},{6,7},{7,8},{8,9},{9,10},{10,1... | collective-permute-start | bytes 786440 | tf_op jit(solution)/shard_map/while/body/eval_jaxpr/ppermute | solution.py:14
  259.4 4.3 %copy-start = (f32[4,1024,128]{2,1,0:T(8,128)S(1)}, f32[4,1024,128]{2,1,0:T(8,128)}, u32[]{:S(2)}) copy-start(f32[4,1024,128]{2,1,0:T(8,128)} %get-tuple-element.384) | copy-start | bytes 6291460 | tf_op jit(solution)/shard_map/while
  270.0 1.4 copy-start.1
  271.4 11.9 %collective-permute-start = (bf16[1024,128]{1,0:T(8,128)(2,1)S(1)}, bf16[1024,128]{1,0:T(8,128)(2,1)S(1)}, u32[]{:S(2)}, u32[]{:S(2)}) collective-permute-start(bf16[1024,128]{1,0:T(8,128)(2,1)S(1)} %get-tuple-element.380), channel_id=1, source_target_pairs={{0,1},{1,2},{2,3},{3,4},{4,5},{5,6},{6,7},{7,8},{8,9},{9,10},{10,1... | collective-permute-start | bytes 786440 | tf_op jit(solution)/shard_map/while/body/eval_jaxpr/ppermute | solution.py:14
  273.3 18.3 %collective-permute-start.1 = (bf16[1024,128]{1,0:T(8,128)(2,1)S(1)}, bf16[1024,128]{1,0:T(8,128)(2,1)S(1)}, u32[]{:S(2)}, u32[]{:S(2)}) collective-permute-start(bf16[1024,128]{1,0:T(8,128)(2,1)S(1)} %get-tuple-element.381), channel_id=1, source_target_pairs={{0,1},{1,2},{2,3},{3,4},{4,5},{5,6},{6,7},{7,8},{8,9},{9,10},{10,1... | collective-permute-start | bytes 786440 | tf_op jit(solution)/shard_map/while/body/eval_jaxpr/ppermute | solution.py:14
  287.3 4.3 %copy-start = (f32[4,1024,128]{2,1,0:T(8,128)S(1)}, f32[4,1024,128]{2,1,0:T(8,128)}, u32[]{:S(2)}) copy-start(f32[4,1024,128]{2,1,0:T(8,128)} %get-tuple-element.384) | copy-start | bytes 6291460 | tf_op jit(solution)/shard_map/while
  297.9 1.4 copy-start.1
  299.3 11.9 %collective-permute-start = (bf16[1024,128]{1,0:T(8,128)(2,1)S(1)}, bf16[1024,128]{1,0:T(8,128)(2,1)S(1)}, u32[]{:S(2)}, u32[]{:S(2)}) collective-permute-start(bf16[1024,128]{1,0:T(8,128)(2,1)S(1)} %get-tuple-element.380), channel_id=1, source_target_pairs={{0,1},{1,2},{2,3},{3,4},{4,5},{5,6},{6,7},{7,8},{8,9},{9,10},{10,1... | collective-permute-start | bytes 786440 | tf_op jit(solution)/shard_map/while/body/eval_jaxpr/ppermute | solution.py:14
  301.2 18.3 %collective-permute-start.1 = (bf16[1024,128]{1,0:T(8,128)(2,1)S(1)}, bf16[1024,128]{1,0:T(8,128)(2,1)S(1)}, u32[]{:S(2)}, u32[]{:S(2)}) collective-permute-start(bf16[1024,128]{1,0:T(8,128)(2,1)S(1)} %get-tuple-element.381), channel_id=1, source_target_pairs={{0,1},{1,2},{2,3},{3,4},{4,5},{5,6},{6,7},{7,8},{8,9},{9,10},{10,1... | collective-permute-start | bytes 786440 | tf_op jit(solution)/shard_map/while/body/eval_jaxpr/ppermute | solution.py:14
  315.2 4.3 %copy-start = (f32[4,1024,128]{2,1,0:T(8,128)S(1)}, f32[4,1024,128]{2,1,0:T(8,128)}, u32[]{:S(2)}) copy-start(f32[4,1024,128]{2,1,0:T(8,128)} %get-tuple-element.384) | copy-start | bytes 6291460 | tf_op jit(solution)/shard_map/while
  325.8 1.4 copy-start.1
where the time goes:
time: 331 us; the launch traced here: 330 us
  matrix products  123 us (37%)
  other arithmetic  70.3 us (21%)
  waiting for transfers between devices  65.7 us (20%)
  starting transfers between devices  49.6 us (15%)
  local copies, waits for them, and re-layouts  20.1 us (6%)
    dot_general x12, matrix products, attend(): jnp.einsum('hqk,kd->hqd', weights.astype(jnp.bfloat16), value_rows, prefe...  75.5 us
    ppermute x22, waiting for transfers between devices, from_behind(): return lax.ppermute(block, axis, route)  65.7 us
    reduce_sum x12, other arithmetic, attend(): total_new = total_old * factor + jnp.sum(weights, axis=-1)  50.3 us
    ppermute x22, starting transfers between devices, from_behind(): return lax.ppermute(block, axis, route)  49.6 us
    dot_general x12, matrix products, attend(): jnp.einsum('qhd,kd->hqk', shaped, key_rows, preferred_element_type=jnp.fl...  47.2 us
    and x12, other arithmetic, attend(): visible = visible & (key_pos[None, :] >= 0)  15.6 us
    while x77, local copies, waits for them, and re-layouts  15.3 us
  transfers between devices with their start and end apart: 22, of which 11 were waited for; matrix products, arithmetic and copies ran while one was open for 32% of the time, Pallas kernels for 0%

commit v1 on v0

v1 whole, which is shorter than its diff:
```python
import functools
import jax
import jax.numpy as jnp
from jax import lax
from jax.experimental import pallas as pl
from jax.experimental.pallas import tpu as pltpu
from jax.sharding import PartitionSpec as P

HEAD = 128
QHEADS = 4
REACH = 11
TOK = 1024
GROUP = 8
DOCS = 16
ROWS = 2 * TOK
SCALE = HEAD ** -0.5 * 1.4426950408889634
HIDDEN = -1e30
SAFE = 2.0 ** 100
MESH = pl.DeviceIdType.MESH
CONTRACT_LAST = (((1,), (1,)), ((), ()))


def order_of(c):
    row = c // 4
    beside = [row * 4 + (c + turn) % 4 for turn in (1, 3, 2)]
    across = [(place + 4) % 8 for place in [c] + beside]
    arrival = [c, across[0], beside[0], beside[1], across[1], across[2], beside[2], across[3]]
    before = [place for place in arrival if place >= c - 3]
    others = [8 + place for place in arrival if place < c or place >= c + 5]
    return before + others


def events_of(c):
    across = (c + 4) % 8
    row = c // 4
    beside = [row * 4 + (c + turn) % 4 for turn in (1, 3, 2)]
    second = 1 + sum(place >= c - 3 for place in [across] + beside[:2])
    third = second + sum(place >= c - 3 for place in [(place + 4) % 8 for place in beside[:2]] + beside[2:])
    return second, third


def pick(c, options):
    value = options[0]
    for place in range(1, GROUP):
        value = jnp.where(c == place, options[place], value)
    return value


def edges(lengths_ref):
    lane = lax.broadcasted_iota(jnp.int32, (1, HEAD), 1)
    starts = jnp.zeros((1, HEAD), jnp.int32)
    ends = jnp.zeros((1, HEAD), jnp.int32)
    at = jnp.int32(0)
    for doc in range(DOCS):
        starts = jnp.where(lane == doc, at, starts)
        at = at + lengths_ref[doc]
        ends = jnp.where(lane == doc, at, ends)
    return starts, ends


def inside(block, starts, ends):
    positions = block * TOK + lax.broadcasted_iota(jnp.int32, (TOK, HEAD), 0)
    return (positions >= starts) & (positions < ends)


def with_marks(block, key_rows, starts, ends):
    marks = jnp.where(inside(block, starts, ends), 0.0, HIDDEN).astype(jnp.bfloat16)
    return jnp.concatenate([key_rows, marks], axis=1)


def turned(ref):
    pieces = [ref[TOK + part * HEAD:TOK + (part + 1) * HEAD, :] for part in range(TOK // HEAD)]
    ones = jnp.ones((16, TOK), jnp.bfloat16)
    return jnp.concatenate([jnp.concatenate(pieces, axis=1), ones], axis=0)


def block_at(o, c, slot):
    place = slot % GROUP
    own_group = jnp.where(place < c, o, o - 2)
    return jnp.where(slot < GROUP, o - 1, own_group) * GROUP + place


def kernel(outers, lengths_ref, q_ref, k_ref, v_ref, o_ref, worst_ref, window_ref,
           own, slots, wide, top, acc, send_sem, recv_sem, keep_sem):
    o, c = lax.axis_index("outer"), lax.axis_index("inner")
    row, y = c // 4, c % 4
    c_next, c_prev, c_far = row * 4 + (y + 1) % 4, row * 4 + (y + 3) % 4, row * 4 + (y + 2) % 4
    c_over = (c + 4) % 8
    over_next, over_prev, over_far = (c_next + 4) % 8, (c_prev + 4) % 8, (c_far + 4) % 8
    later, earlier = ((o + 1) % outers, c), ((o + outers - 1) % outers, c)
    at_next, at_prev, at_over = (o, c_next), (o, c_prev), (o, c_over)

    barrier = pltpu.get_barrier_semaphore()
    for device in (later, earlier, at_next, at_prev, at_over):
        pl.semaphore_signal(barrier, inc=1, device_id=device, device_id_type=MESH)
    own[0:TOK, :] = k_ref[...]
    values_t = v_ref[...].T
    for part in range(TOK // HEAD):
        own[TOK + part * HEAD:TOK + (part + 1) * HEAD, :] = values_t[:, part * HEAD:(part + 1) * HEAD]
    pl.semaphore_wait(barrier, 5)

    def copy(source, slot, device, send, part=None):
        if part is None:
            target, recv = slots.at[slot], recv_sem.at[slot]
        else:
            rows = pl.ds(part * TOK, TOK)
            source, target = source.at[rows, :], slots.at[slot, rows, :]
            recv = recv_sem.at[slot if part == 0 else 16]
        return pltpu.make_async_remote_copy(
            src_ref=source, dst_ref=target, send_sem=send_sem.at[send], recv_sem=recv,
            device_id=device, device_id_type=MESH)

    def pass_on(slot, send):
        @pl.when(slot < c)
        def _():
            copy(slots.at[slot], GROUP + slot, earlier, send).start()

        @pl.when(slot >= c + 5)
        def _():
            copy(slots.at[slot], GROUP + slot, later, send).start()

    def passed(slot, send):
        @pl.when((slot < c) | (slot >= c + 5))
        def _():
            copy(slots.at[slot], GROUP + slot, earlier, send).wait_send()

    def arrived(slot, part=None):
        copy(slots.at[slot] if part is None else slots.at[slot], slot, later, 0, part).wait_recv()

    copy(own, c, later, 0).start()

    starts, ends = edges(lengths_ref)
    here = o * GROUP + c
    marks = jnp.where(inside(here, starts, ends), 1.0, 0.0).astype(jnp.bfloat16)
    for head in range(QHEADS):
        wide[head * TOK:(head + 1) * TOK, 0:HEAD] = q_ref[:, head * HEAD:(head + 1) * HEAD]
        wide[head * TOK:(head + 1) * TOK, HEAD:2 * HEAD] = marks

    own_keys = with_marks(here, own[0:TOK, :], starts, ends)
    own_values = turned(own)
    half = TOK // 2
    for head in range(QHEADS):
        for first in (0, half):
            depth = first + half
            at = head * TOK + first
            scores = lax.dot_general(
                own_keys[0:depth], wide[at:at + half, :], CONTRACT_LAST,
                preferred_element_type=jnp.float32)
            key_at = lax.broadcasted_iota(jnp.int32, (depth, half), 0)
            query_at = lax.broadcasted_iota(jnp.int32, (depth, half), 1) + first
            scores = jnp.where(key_at <= query_at, scores * SCALE, HIDDEN)
            highest = jnp.max(scores, axis=0, keepdims=True)
            top[0:1, at:at + half] = highest
            weights = jnp.exp2(scores - highest).astype(jnp.bfloat16)
            acc[:, at:at + half] = jnp.dot(
                own_values[:, 0:depth], weights, preferred_element_type=jnp.float32)

    orders = [order_of(place) for place in range(GROUP)]
    low = pick(c, [sum(slot << (4 * step) for step, slot in enumerate(order[:6])) for order in orders])
    high = pick(c, [sum(slot << (4 * step) for step, slot in enumerate(order[6:])) for order in orders])

    second = pick(c, [events_of(place)[0] for place in range(GROUP)])
    third = pick(c, [events_of(place)[1] for place in range(GROUP)])

    def step_slot(step):
        return jnp.where(
            step < 6,
            lax.shift_right_logical(low, 4 * jnp.minimum(step, 5)) & 15,
            lax.shift_right_logical(high, 4 * jnp.maximum(step - 6, 0)) & 15)

    def work(step, _):
        @pl.when(step == 0)
        def _():
            arrived(c)
            copy(slots.at[c], c, at_next, 1).start()
            copy(slots.at[c], c, at_prev, 2).start()
            copy(slots.at[c], c, at_over, 3).start()

        @pl.when(step == 1)
        def _():
            for slot in (c_over, c_next, c_prev):
                arrived(slot)
            copy(slots.at[c_over], c_over, at_next, 4).start()
            copy(slots.at[c_over], c_over, at_prev, 5).start()
            copy(slots.at[c_prev], c_prev, at_next, 6, 0).start()
            copy(slots.at[c_next], c_next, at_prev, 7, 1).start()
            for send, slot in enumerate((c_over, c_next, c_prev)):
                pass_on(slot, 9 + send)

        @pl.when(step == second)
        def _():
            for slot in (over_next, over_prev):
                arrived(slot)
            arrived(c_far, 0)
            arrived(c_far, 1)
            copy(slots.at[c_far], c_far, at_over, 8).start()
            for send, slot in enumerate((over_next, over_prev, c_far)):
                pass_on(slot, 12 + send)

        @pl.when(step == third)
        def _():
            arrived(over_far)
            pass_on(over_far, 15)

        slot = step_slot(step)

        @pl.when(slot >= GROUP)
        def _():
            arrived(slot)

        pltpu.make_async_copy(slots.at[slot], window_ref.at[step], keep_sem.at[step]).start()
        keys = with_marks(block_at(o, c, slot), slots[slot, 0:TOK, :], starts, ends)
        values = turned(slots.at[slot])
        for head in range(QHEADS):
            columns = slice(head * TOK, (head + 1) * TOK)
            scores = lax.dot_general(
                keys, wide[columns, :], CONTRACT_LAST, preferred_element_type=jnp.float32)
            weights = jnp.exp2(scores * SCALE - top[0:1, columns]).astype(jnp.bfloat16)
            acc[:, columns] += jnp.dot(values, weights, preferred_element_type=jnp.float32)
        return 0

    lax.fori_loop(0, REACH, work, 0)

    worst = jnp.zeros((1, TOK), jnp.float32)
    for head in range(QHEADS):
        columns = slice(head * TOK, (head + 1) * TOK)
        total = acc[HEAD:HEAD + 1, columns]
        worst = jnp.where(total < SAFE, worst, 1.0)
        o_ref[:, head * HEAD:(head + 1) * HEAD] = (acc[0:HEAD, columns] / total).T.astype(jnp.bfloat16)
    worst_ref[...] = jnp.broadcast_to(jnp.max(worst, axis=1, keepdims=True), (8, HEAD))

    copy(own, c, later, 0).wait_send()
    for send, slot, part in ((1, c, None), (2, c, None), (3, c, None), (4, c_over, None),
                             (5, c_over, None), (6, c_prev, 0), (7, c_next, 1), (8, c_far, None)):
        copy(slots.at[slot], slot, at_next, send, part).wait_send()
    for send, slot in enumerate((c_over, c_next, c_prev, over_next, over_prev, c_far, over_far)):
        passed(slot, 9 + send)

    def kept(step, _):
        pltpu.make_async_copy(slots.at[0], window_ref.at[step], keep_sem.at[step]).wait()
        return 0

    lax.fori_loop(0, REACH, kept, 0)


def repair(outer_size, worst_ref, lengths_ref, place_ref, q_hbm, k_hbm, v_hbm, window_hbm, given, out_hbm,
           queries, block_rows, values_t, marks, result, top, acc):
    @pl.when(worst_ref[0, 0] > 0.0)
    def _():
        o, c = place_ref[0], place_ref[1]
        here = o * GROUP + c
        starts, ends = edges(lengths_ref)
        pltpu.sync_copy(q_hbm, queries)
        marks[...] = jnp.where(inside(here, starts, ends), 1.0, 0.0).astype(jnp.bfloat16)
        acc[...] = jnp.zeros_like(acc)
        top[...] = jnp.full_like(top, HIDDEN)

        def scan(keys, head_values, own_block):
            for head in range(QHEADS):
                columns = slice(head * TOK, (head + 1) * TOK)
                wide = jnp.concatenate([queries[:, head * HEAD:(head + 1) * HEAD], marks[...]], axis=1)
                scores = lax.dot_general(keys, wide, CONTRACT_LAST, preferred_element_type=jnp.float32)
                scores = scores * SCALE
                if own_block:
                    key_at = lax.broadcasted_iota(jnp.int32, (TOK, TOK), 0)
                    query_at = lax.broadcasted_iota(jnp.int32, (TOK, TOK), 1)
                    scores = jnp.where(key_at <= query_at, scores, HIDDEN)
                old = top[0:1, columns]
                new = jnp.maximum(old, jnp.max(scores, axis=0, keepdims=True))
                top[0:1, columns] = new
                weights = jnp.exp2(scores - new).astype(jnp.bfloat16)
                acc[:, columns] = acc[:, columns] * jnp.exp2(old - new) + jnp.dot(
                    head_values, weights, preferred_element_type=jnp.float32)

        pltpu.sync_copy(k_hbm, block_rows.at[0:TOK, :])
        pltpu.sync_copy(v_hbm, block_rows.at[TOK:ROWS, :])
        values_t[...] = block_rows[TOK:ROWS, :].T
        ones = jnp.ones((16, TOK), jnp.bfloat16)
        scan(with_marks(here, block_rows[0:TOK, :], starts, ends),
             jnp.concatenate([values_t[...], ones], axis=0), True)

        def one(step, _):
            pltpu.sync_copy(window_hbm.at[step], block_rows)
            block = here - place_ref[2 + step]
            scan(with_marks(block, block_rows[0:TOK, :], starts, ends), turned(block_rows), False)
            return 0

        lax.fori_loop(0, REACH, one, 0)
        for head in range(QHEADS):
            columns = slice(head * TOK, (head + 1) * TOK)
            result[:, head * HEAD:(head + 1) * HEAD] = (
                acc[0:HEAD, columns] / acc[HEAD:HEAD + 1, columns]).T.astype(jnp.bfloat16)
        pltpu.sync_copy(result, out_hbm)


def distances(c):
    return [8 + c - slot if slot < 8 else (c - slot + 8 if slot - 8 < c else 16 + c - (slot - 8))
            for slot in order_of(c)]


def per_device(outers, queries, keys, values, doc_lengths):
    vmem = pl.BlockSpec(memory_space=pltpu.VMEM)
    smem = pl.BlockSpec(memory_space=pltpu.SMEM)
    anywhere = pl.BlockSpec(memory_space=pl.ANY)
    out_shape = jax.ShapeDtypeStruct((TOK, QHEADS * HEAD), jnp.bfloat16)
    first, worst, window = pl.pallas_call(
        functools.partial(kernel, outers),
        out_shape=(out_shape, jax.ShapeDtypeStruct((8, HEAD), jnp.float32),
                   jax.ShapeDtypeStruct((REACH, ROWS, HEAD), jnp.bfloat16)),
        in_specs=[smem, vmem, vmem, vmem],
        out_specs=(vmem, vmem, anywhere),
        scratch_shapes=[
            pltpu.VMEM((ROWS, HEAD), jnp.bfloat16),
            pltpu.VMEM((16, ROWS, HEAD), jnp.bfloat16),
            pltpu.VMEM((QHEADS * TOK, 2 * HEAD), jnp.bfloat16),
            pltpu.VMEM((8, QHEADS * TOK), jnp.float32),
            pltpu.VMEM((HEAD + 16, QHEADS * TOK), jnp.float32),
            pltpu.SemaphoreType.DMA((16,)),
            pltpu.SemaphoreType.DMA((17,)),
            pltpu.SemaphoreType.DMA((REACH,)),
        ],
        compiler_params=pltpu.CompilerParams(
            collective_id=0, has_side_effects=True, vmem_limit_bytes=56 << 20),
        cost_estimate=pl.CostEstimate(
            flops=4 * 12 * QHEADS * TOK * TOK * HEAD, bytes_accessed=12 << 20,
            transcendentals=12 * QHEADS * TOK * TOK),
    )(doc_lengths, queries, keys, values)
    o, c = lax.axis_index("outer"), lax.axis_index("inner")
    table = jnp.array([distances(place) for place in range(GROUP)], jnp.int32)
    place = jnp.concatenate([jnp.stack([o, c]).astype(jnp.int32), table[c]])
    return pl.pallas_call(
        functools.partial(repair, outers),
        out_shape=out_shape,
        in_specs=[smem, smem, smem] + [anywhere] * 5,
        out_specs=anywhere,
        input_output_aliases={7: 0},
        scratch_shapes=[
            pltpu.VMEM((TOK, QHEADS * HEAD), jnp.bfloat16),
            pltpu.VMEM((ROWS, HEAD), jnp.bfloat16),
            pltpu.VMEM((HEAD, TOK), jnp.bfloat16),
            pltpu.VMEM((TOK, HEAD), jnp.bfloat16),
            pltpu.VMEM((TOK, QHEADS * HEAD), jnp.bfloat16),
            pltpu.VMEM((8, QHEADS * TOK), jnp.float32),
            pltpu.VMEM((HEAD + 16, QHEADS * TOK), jnp.float32),
        ],
        compiler_params=pltpu.CompilerParams(vmem_limit_bytes=56 << 20),
    )(worst, doc_lengths, place, queries, keys, values, window, first)


def solution(mesh):
    rows = P(("outer", "inner"), None)
    return jax.shard_map(
        functools.partial(per_device, mesh.shape["outer"]),
        mesh=mesh,
        in_specs=(rows, rows, rows, P()),
        out_specs=rows,
        check_vma=False,
    )
```

time: 331 us -> 102 us (0.31)
  the two profiles are of different devices: /device:TPU:64 before, /device:TPU:31 now
where the time goes in v1:
time: 102 us
  Pallas kernels  98.2 us (96%)
  local copies, waits for them, and re-layouts  2.95 us (3%)
    pallas_call x1, Pallas kernels, per_device(): pl.pallas_call(functools.partial(kernel, outers), out_shape=(out_shape, j...  97.3 us
    unnamed x1, local copies, waits for them, and re-layouts  2.26 us

profile of v1, /device:TPU:31, one launch (start us, length us, event | category | flops | bytes accessed | tf_op | source)
XLA Modules:
  0.0 101.8 jit_solution(9625063747988424651)
XLA Ops:
  0.0 0.7 dynamic-slice_bitcast_fusion
  0.7 0.6 pad_add_fusion.place_ref
  1.3 97.3 %shard_map.55 = (bf16[1024,512]{1,0:T(8,128)(2,1)}, f32[8,128]{1,0:T(8,128)}, bf16[11,2048,128]{2,1,0:T(8,128)(2,1)}) custom-call(s32[16]{0:T(128)} %lengths_ref.3, bf16[1024,512]{1,0:T(8,128)(2,1)} %q_hbm.1, bf16[1024,128]{1,0:T(8,128)(2,1)} %k_hbm.1, bf16[1024,128]{1,0:T(8,128)(2,1)} %v_hbm.1), custom_call_target="tpu_custom_call" | custom-call | flops 25769803776 | bytes 12582912 | tf_op jit(solution)/shard_map/pallas_call | solution.py:306
  98.6 0.9 shard_map.56
  99.6 2.3 %copy.9 = bf16[1024,512]{1,0:T(8,128)(2,1)} copy(bf16[1024,512]{1,0:T(8,128)(2,1)} %shard_map.56) | data formatting | bytes 2097152

commit v2 on v1

v2 whole, which is shorter than its diff:
```python
import functools
import jax
import jax.numpy as jnp
from jax import lax
from jax.experimental import pallas as pl
from jax.experimental.pallas import tpu as pltpu
from jax.sharding import PartitionSpec as P

HEAD = 128
QHEADS = 4
REACH = 11
TOK = 1024
GROUP = 8
DOCS = 16
ROWS = 2 * TOK
SCALE = HEAD ** -0.5 * 1.4426950408889634
HIDDEN = -1e30
SAFE = 2.0 ** 100
MESH = pl.DeviceIdType.MESH
CONTRACT_LAST = (((1,), (1,)), ((), ()))


SENDS = [
    [606160960, 304096322, 268512322, 415672322, 339879936, 281485708, 667922566, 667871134, 869150852, 659279509, 0, 0, 0, 0, 0],
    [840987714, 136342594, 841053248, 136408128, 436218880, 818295810, 440604311, 440538773, 198109712, 198142084, 898429192, 822700694, 193727291, 2873, 0],
    [610355392, 878733506, 442574016, 272836742, 605103298, 605038724, 411411095, 437280802, 357256985, 931942171, 285781818, 0, 0, 0, 0],
    [845182146, 979374274, 140534978, 440537121, 974154389, 193849610, 881071897, 952623105, 198175512, 444887437, 98470847, 0, 0, 0, 0],
    [614549824, 882993472, 344270146, 609396032, 344207757, 609432898, 294466726, 441590552, 290172860, 437379238, 0, 0, 0, 0, 0],
    [983590210, 849350978, 144733506, 139638024, 898495652, 198108327, 844261774, 902764447, 135303203, 100789148, 100725794, 98470847, 0, 0, 0],
    [618744256, 887185856, 887120322, 281422220, 613785998, 613730336, 298829858, 298723726, 277213086, 277114780, 10771, 0, 0, 0, 0],
    [148927938, 148993472, 144029070, 902804876, 907088168, 907048232, 982868894, 444960935, 436302882, 978479633, 105090181, 0, 0, 0, 0],
    [622938688, 958427714, 320941634, 352858640, 387981840, 357282322, 303112589, 424298663, 609397926, 370177819, 298722206, 23817, 0, 0, 0],
    [857805376, 153185858, 924870208, 319320726, 840012207, 894137244, 907047707, 113697692, 113749124, 109350155, 0, 0, 0, 0, 0],
    [627133120, 895513282, 895578816, 424356502, 622404246, 622340756, 428651156, 320351000, 285815579, 784771337, 420033040, 303081738, 613806640, 18729, 0],
    [157378240, 157312706, 152675988, 898495257, 323708071, 143977240, 911369248, 911412623, 3469, 0, 0, 0, 0, 0, 0],
    [631327552, 899707714, 899773248, 329263896, 294466328, 361581237, 290075418, 348598932, 626730281, 962284081, 957958707, 11562, 0, 0, 0],
    [161507138, 161572672, 156935962, 915731357, 915771823, 152625813, 902787732, 920086198, 844326580, 113675663, 0, 0, 0, 0, 0],
    [635521984, 836856768, 903967680, 971072448, 298791838, 622441372, 630999866, 298725905, 622375442, 957948699, 819342236, 424323998, 966615470, 886530347, 962259372],
    [165680066, 852979119, 152694189, 924324664, 924411308, 122334739, 848629399, 0, 0, 0, 0, 0, 0, 0, 0],
]
COUNTS = [
    [794754, 2921032, 4518732, 5326034, 5326100, 5326100],
    [2654728, 2929354, 4522892, 5850322, 7190168, 7190235],
    [1589508, 3723977, 4785168, 5858578, 5858710, 5858710],
    [1597830, 2658887, 3990283, 5321809, 5858645, 5858710],
    [1327364, 2925127, 4522893, 5326098, 5326100, 5326100],
    [1859974, 3453576, 4527054, 6116627, 6391319, 6391320],
    [1597830, 3723977, 5055503, 5592340, 5592405, 5592405],
    [1327364, 2920966, 4260749, 5317713, 5854549, 5858710],
    [1589508, 3195594, 4522893, 6124883, 6125015, 6125015],
    [1597830, 2392582, 3723978, 4522958, 5325970, 5326100],
    [1597830, 3723977, 5584016, 6657558, 7190234, 7190235],
    [1327364, 2396678, 3195659, 3728268, 4527184, 4527185],
    [1597830, 3990282, 5317712, 6125014, 6125015, 6125015],
    [1327364, 2392583, 3457674, 4523022, 5059730, 5326100],
    [2130440, 4518731, 6382867, 7989018, 7989150, 7989150],
    [532610, 2388356, 2929290, 3461963, 3728269, 3728270],
]
STEPS = [
    [13834480, 13128189, 257471],
    [13843568, 10168773, 250815],
    [5705265, 13397906, 227647],
    [9906737, 6043654, 214014],
    [14326898, 12727679, 216536],
    [5807346, 201223, 214005],
    [6073907, 12930066, 236918],
    [6260403, 9542674, 217206],
    [9264692, 12883383, 241378],
    [6520180, 988571, 241218],
    [13868853, 10631302, 225979],
    [6580021, 14593588, 205051],
    [12008822, 15156010, 245303],
    [2808310, 9883227, 15924],
    [15617975, 6968716, 237101],
    [3002295, 1549622, 237432],
]
OWN = 16
PARTS = 17


def pick(kind, options):
    value = options[0]
    for other in range(1, len(options)):
        value = jnp.where(kind == other, options[other], value)
    return value


def words_for(kind, table):
    return [pick(kind, [words[at] for words in table]) for at in range(len(table[0]))]


def unpack(words, index, per_word, bits):
    word = words[0]
    for at in range(1, len(words)):
        word = jnp.where(index // per_word == at, words[at], word)
    return lax.shift_right_logical(word, bits * (index % per_word)) & ((1 << bits) - 1)


def edges(lengths_ref):
    lane = lax.broadcasted_iota(jnp.int32, (1, HEAD), 1)
    starts = jnp.zeros((1, HEAD), jnp.int32)
    ends = jnp.zeros((1, HEAD), jnp.int32)
    at = jnp.int32(0)
    for doc in range(DOCS):
        starts = jnp.where(lane == doc, at, starts)
        at = at + lengths_ref[doc]
        ends = jnp.where(lane == doc, at, ends)
    return starts, ends


def inside(block, starts, ends):
    positions = block * TOK + lax.broadcasted_iota(jnp.int32, (TOK, HEAD), 0)
    return (positions >= starts) & (positions < ends)


def with_marks(block, key_rows, starts, ends):
    marks = jnp.where(inside(block, starts, ends), 0.0, HIDDEN).astype(jnp.bfloat16)
    return jnp.concatenate([key_rows, marks], axis=1)


def turned(ref):
    pieces = [ref[TOK + part * HEAD:TOK + (part + 1) * HEAD, :] for part in range(TOK // HEAD)]
    ones = jnp.ones((16, TOK), jnp.bfloat16)
    return jnp.concatenate([jnp.concatenate(pieces, axis=1), ones], axis=0)


def block_at(o, c, slot):
    place = slot % GROUP
    own_group = jnp.where(place < c, o, o - 2)
    return jnp.where(slot < GROUP, o - 1, own_group) * GROUP + place


def kernel(outers, lengths_ref, q_ref, k_ref, v_ref, o_ref, worst_ref, window_ref,
           slots, wide, top, acc, send_sem, recv_sem, keep_sem):
    o, c = lax.axis_index("outer"), lax.axis_index("inner")
    core, pair = o % 2, o // 2
    row, y = c // 4, c % 4
    pairs = outers // 2
    after, ahead = (pair + 1) % pairs, (pair + pairs - 1) % pairs
    c_next, c_prev, c_over = row * 4 + (y + 1) % 4, row * 4 + (y + 3) % 4, (c + 4) % 8
    mate = pair * 2 + 1 - core

    barrier = pltpu.get_barrier_semaphore()
    partners = [(mate, c)]
    for there in (0, 1):
        partners += [(after * 2 + there, c), (ahead * 2 + there, c)]
        partners += [(pair * 2 + there, place) for place in (c_next, c_prev, c_over)]
    for device in partners:
        pl.semaphore_signal(barrier, inc=1, device_id=device, device_id_type=MESH)
    slots[OWN, 0:TOK, :] = k_ref[...]
    values_t = v_ref[...].T
    for part in range(TOK // HEAD):
        slots[OWN, TOK + part * HEAD:TOK + (part + 1) * HEAD, :] = values_t[:, part * HEAD:(part + 1) * HEAD]
    kind = c * 2 + core
    sends, counts, steps = (words_for(kind, table) for table in (SENDS, COUNTS, STEPS))
    pl.semaphore_wait(barrier, len(partners))

    def copy(source, target, part, send, device):
        rows = pl.ds(pl.multiple_of(part * TOK, TOK), TOK)
        return pltpu.make_async_remote_copy(
            src_ref=slots.at[source, rows, :], dst_ref=slots.at[target, rows, :],
            send_sem=send_sem.at[send], recv_sem=recv_sem.at[target * 2 + part],
            device_id=device, device_id_type=MESH)

    def send(index, _):
        code = unpack(sends, index, 2, 15)
        waits, part, source, target = code & 1, (code // 2) & 1, (code // 4) & 31, (code // 128) & 15
        way, there = (code // 2048) & 7, code // 16384

        @pl.when(waits == 1)
        def _():
            copy(source, source, part, 0, (mate, c)).wait_recv()

        to_pair = jnp.where(way == 2, after, jnp.where(way == 3, ahead, pair))
        to_place = jnp.where(way == 4, c_next, jnp.where(way == 5, c_prev, jnp.where(way == 6, c_over, c)))
        copy(source, target, part, index, (to_pair * 2 + there, to_place)).start()
        return 0

    def send_upto(turn, done):
        upto = unpack(counts, turn, 4, 6)
        lax.fori_loop(done, upto, send, 0)
        return upto

    done = send_upto(0, 0)

    starts, ends = edges(lengths_ref)
    here = o * GROUP + c
    marks = jnp.where(inside(here, starts, ends), 1.0, 0.0).astype(jnp.bfloat16)
    for head in range(QHEADS):
        wide[head * TOK:(head + 1) * TOK, 0:HEAD] = q_ref[:, head * HEAD:(head + 1) * HEAD]
        wide[head * TOK:(head + 1) * TOK, HEAD:2 * HEAD] = marks

    own_keys = with_marks(here, slots[OWN, 0:TOK, :], starts, ends)
    own_values = turned(slots.at[OWN])
    half = TOK // 2
    for head in range(QHEADS):
        if head == 2:
            done = send_upto(1, done)
        for first in (0, half):
            depth = first + half
            at = head * TOK + first
            scores = lax.dot_general(
                own_keys[0:depth], wide[at:at + half, :], CONTRACT_LAST,
                preferred_element_type=jnp.float32)
            key_at = lax.broadcasted_iota(jnp.int32, (depth, half), 0)
            query_at = lax.broadcasted_iota(jnp.int32, (depth, half), 1) + first
            scores = jnp.where(key_at <= query_at, scores * SCALE, HIDDEN)
            highest = jnp.max(scores, axis=0, keepdims=True)
            top[0:1, at:at + half] = highest
            weights = jnp.exp2(scores - highest).astype(jnp.bfloat16)
            acc[:, at:at + half] = jnp.dot(
                own_values[:, 0:depth], weights, preferred_element_type=jnp.float32)

    def work(step, done):
        done = send_upto(2 + 2 * step, done)
        code = unpack(steps, step, 4, 6)
        slot = code & 15
        for part in (0, 1):
            @pl.when((code // (16 << part)) & 1 == 1)
            def _():
                copy(slot, slot, part, 0, (mate, c)).wait_recv()

        pltpu.make_async_copy(slots.at[slot], window_ref.at[step], keep_sem.at[step]).start()
        keys = with_marks(block_at(o, c, slot), slots[slot, 0:TOK, :], starts, ends)
        values = turned(slots.at[slot])
        for head in range(QHEADS):
            if head == 2:
                done = send_upto(3 + 2 * step, done)
            columns = slice(head * TOK, (head + 1) * TOK)
            scores = lax.dot_general(
                keys, wide[columns, :], CONTRACT_LAST, preferred_element_type=jnp.float32)
            weights = jnp.exp2(scores * SCALE - top[0:1, columns]).astype(jnp.bfloat16)
            acc[:, columns] += jnp.dot(values, weights, preferred_element_type=jnp.float32)
        return done

    done = lax.fori_loop(0, REACH, work, done)

    worst = jnp.zeros((1, TOK), jnp.float32)
    for head in range(QHEADS):
        columns = slice(head * TOK, (head + 1) * TOK)
        total = acc[HEAD:HEAD + 1, columns]
        worst = jnp.where(total < SAFE, worst, 1.0)
        o_ref[:, head * HEAD:(head + 1) * HEAD] = (acc[0:HEAD, columns] / total).T.astype(jnp.bfloat16)
    worst_ref[...] = jnp.broadcast_to(jnp.max(worst, axis=1, keepdims=True), (8, HEAD))

    def sent(index, _):
        copy(OWN, 0, 0, index, (mate, c)).wait_send()
        return 0

    def kept(step, _):
        pltpu.make_async_copy(slots.at[0], window_ref.at[step], keep_sem.at[step]).wait()
        return 0

    lax.fori_loop(0, done, sent, 0)
    lax.fori_loop(0, REACH, kept, 0)


def repair(outer_size, worst_ref, lengths_ref, place_ref, q_hbm, k_hbm, v_hbm, window_hbm, given, out_hbm,
           queries, block_rows, values_t, marks, result, top, acc, pass_sem):
    @pl.when(worst_ref[0, 0] <= 0.0)
    def _():
        chunk = TOK // 4
        parts = [pl.ds(part * chunk, chunk) for part in range(4)]
        reads = [pltpu.make_async_copy(given.at[rows, :], result.at[rows, :], pass_sem.at[0, part])
                 for part, rows in enumerate(parts)]
        writes = [pltpu.make_async_copy(result.at[rows, :], out_hbm.at[rows, :], pass_sem.at[1, part])
                  for part, rows in enumerate(parts)]
        for read in reads:
            read.start()
        for read, write in zip(reads, writes):
            read.wait()
            write.start()
        for write in writes:
            write.wait()

    @pl.when(worst_ref[0, 0] > 0.0)
    def _():
        o, c = place_ref[0], place_ref[1]
        here = o * GROUP + c
        starts, ends = edges(lengths_ref)
        pltpu.sync_copy(q_hbm, queries)
        marks[...] = jnp.where(inside(here, starts, ends), 1.0, 0.0).astype(jnp.bfloat16)
        acc[...] = jnp.zeros_like(acc)
        top[...] = jnp.full_like(top, HIDDEN)

        def scan(keys, head_values, own_block):
            for head in range(QHEADS):
                columns = slice(head * TOK, (head + 1) * TOK)
                wide = jnp.concatenate([queries[:, head * HEAD:(head + 1) * HEAD], marks[...]], axis=1)
                scores = lax.dot_general(keys, wide, CONTRACT_LAST, preferred_element_type=jnp.float32)
                scores = scores * SCALE
                if own_block:
                    key_at = lax.broadcasted_iota(jnp.int32, (TOK, TOK), 0)
                    query_at = lax.broadcasted_iota(jnp.int32, (TOK, TOK), 1)
                    scores = jnp.where(key_at <= query_at, scores, HIDDEN)
                old = top[0:1, columns]
                new = jnp.maximum(old, jnp.max(scores, axis=0, keepdims=True))
                top[0:1, columns] = new
                weights = jnp.exp2(scores - new).astype(jnp.bfloat16)
                acc[:, columns] = acc[:, columns] * jnp.exp2(old - new) + jnp.dot(
                    head_values, weights, preferred_element_type=jnp.float32)

        pltpu.sync_copy(k_hbm, block_rows.at[0:TOK, :])
        pltpu.sync_copy(v_hbm, block_rows.at[TOK:ROWS, :])
        values_t[...] = block_rows[TOK:ROWS, :].T
        ones = jnp.ones((16, TOK), jnp.bfloat16)
        scan(with_marks(here, block_rows[0:TOK, :], starts, ends),
             jnp.concatenate([values_t[...], ones], axis=0), True)

        def one(step, _):
            pltpu.sync_copy(window_hbm.at[step], block_rows)
            block = here - place_ref[2 + step]
            scan(with_marks(block, block_rows[0:TOK, :], starts, ends), turned(block_rows), False)
            return 0

        lax.fori_loop(0, REACH, one, 0)
        for head in range(QHEADS):
            columns = slice(head * TOK, (head + 1) * TOK)
            result[:, head * HEAD:(head + 1) * HEAD] = (
                acc[0:HEAD, columns] / acc[HEAD:HEAD + 1, columns]).T.astype(jnp.bfloat16)
        pltpu.sync_copy(result, out_hbm)


def distances(kind):
    c = kind // 2
    codes = [(STEPS[kind][step // 4] >> (6 * (step % 4))) & 15 for step in range(REACH)]
    return [8 + c - slot if slot < 8 else (c - slot + 8 if slot - 8 < c else 16 + c - (slot - 8))
            for slot in codes]


def per_device(outers, queries, keys, values, doc_lengths):
    vmem = pl.BlockSpec(memory_space=pltpu.VMEM)
    smem = pl.BlockSpec(memory_space=pltpu.SMEM)
    anywhere = pl.BlockSpec(memory_space=pl.ANY)
    out_shape = jax.ShapeDtypeStruct((TOK, QHEADS * HEAD), jnp.bfloat16)
    first, worst, window = pl.pallas_call(
        functools.partial(kernel, outers),
        out_shape=(out_shape, jax.ShapeDtypeStruct((8, HEAD), jnp.float32),
                   jax.ShapeDtypeStruct((REACH, ROWS, HEAD), jnp.bfloat16)),
        in_specs=[smem, vmem, vmem, vmem],
        out_specs=(vmem, vmem, anywhere),
        scratch_shapes=[
            pltpu.VMEM((PARTS, ROWS, HEAD), jnp.bfloat16),
            pltpu.VMEM((QHEADS * TOK, 2 * HEAD), jnp.bfloat16),
            pltpu.VMEM((8, QHEADS * TOK), jnp.float32),
            pltpu.VMEM((HEAD + 16, QHEADS * TOK), jnp.float32),
            pltpu.SemaphoreType.DMA((2 * len(SENDS[0]),)),
            pltpu.SemaphoreType.DMA((2 * OWN,)),
            pltpu.SemaphoreType.DMA((REACH,)),
        ],
        compiler_params=pltpu.CompilerParams(
            collective_id=0, has_side_effects=True, vmem_limit_bytes=56 << 20),
        cost_estimate=pl.CostEstimate(
            flops=4 * 12 * QHEADS * TOK * TOK * HEAD, bytes_accessed=12 << 20,
            transcendentals=12 * QHEADS * TOK * TOK),
    )(doc_lengths, queries, keys, values)
    o, c = lax.axis_index("outer"), lax.axis_index("inner")
    table = jnp.array([distances(kind) for kind in range(2 * GROUP)], jnp.int32)
    place = jnp.concatenate([jnp.stack([o, c]).astype(jnp.int32), table[c * 2 + o % 2]])
    return pl.pallas_call(
        functools.partial(repair, outers),
        out_shape=out_shape,
        in_specs=[smem, smem, smem] + [anywhere] * 5,
        out_specs=anywhere,
        scratch_shapes=[
            pltpu.VMEM((TOK, QHEADS * HEAD), jnp.bfloat16),
            pltpu.VMEM((ROWS, HEAD), jnp.bfloat16),
            pltpu.VMEM((HEAD, TOK), jnp.bfloat16),
            pltpu.VMEM((TOK, HEAD), jnp.bfloat16),
            pltpu.VMEM((TOK, QHEADS * HEAD), jnp.bfloat16),
            pltpu.VMEM((8, QHEADS * TOK), jnp.float32),
            pltpu.VMEM((HEAD + 16, QHEADS * TOK), jnp.float32),
            pltpu.SemaphoreType.DMA((2, 4)),
        ],
        compiler_params=pltpu.CompilerParams(vmem_limit_bytes=56 << 20),
    )(worst, doc_lengths, place, queries, keys, values, window, first)


def solution(mesh):
    rows = P(("outer", "inner"), None)
    return jax.shard_map(
        functools.partial(per_device, mesh.shape["outer"]),
        mesh=mesh,
        in_specs=(rows, rows, rows, P()),
        out_specs=rows,
        check_vma=False,
    )
```

time: 102 us -> 85.8 us (0.84)
  the two profiles are of different devices: /device:TPU:31 before, /device:TPU:40 now
where the time goes in v2:
time: 85.8 us; the launch traced here: 85.5 us
  Pallas kernels  84 us (98%)
    pallas_call x1, Pallas kernels, per_device(): pl.pallas_call(functools.partial(kernel, outers), out_shape=(out_shape, j...  81.3 us
    pallas_call x1, Pallas kernels, per_device(): pl.pallas_call(functools.partial(repair, outers), out_shape=out_shape, in...  2.73 us

profile of v2, /device:TPU:40, one launch (start us, length us, event | category | flops | bytes accessed | tf_op | source)
XLA Modules:
  0.0 85.5 jit_solution(16979575868633597715)
XLA Ops:
  0.0 0.7 dynamic-slice_bitcast_fusion
  0.7 0.6 pad_add_fusion.place_ref
  1.3 81.3 %shard_map.55 = (bf16[1024,512]{1,0:T(8,128)(2,1)}, f32[8,128]{1,0:T(8,128)}, bf16[11,2048,128]{2,1,0:T(8,128)(2,1)}) custom-call(s32[16]{0:T(128)} %lengths_ref.3, bf16[1024,512]{1,0:T(8,128)(2,1)} %q_hbm.1, bf16[1024,128]{1,0:T(8,128)(2,1)} %k_hbm.1, bf16[1024,128]{1,0:T(8,128)(2,1)} %v_hbm.1), custom_call_target="tpu_custom_call" | custom-call | flops 25769803776 | bytes 12582912 | tf_op jit(solution)/shard_map/pallas_call | solution.py:336
  82.7 2.7 %shard_map.56 = bf16[1024,512]{1,0:T(8,128)(2,1)} custom-call(f32[8,128]{1,0:T(8,128)} %get-tuple-element.8.worst_ref, s32[16]{0:T(128)} %lengths_ref.3, s32[13]{0:T(128)} %pad_add_fusion.place_ref, bf16[1024,512]{1,0:T(8,128)(2,1)} %q_hbm.1, bf16[1024,128]{1,0:T(8,128)(2,1)} %k_hbm.1, bf16[1024,128]{1,0:T(8,128)(2,1)} %v_hbm.1, ...), custom_call_target="tpu_custom_call" | custom-call | tf_op jit(solution)/shard_map/pallas_call | solution.py:360

commit v3 on v2

--- a/solution.py
+++ b/solution.py
@@ -255,7 +255,7 @@
     lax.fori_loop(0, REACH, kept, 0)
 
 
-def repair(outer_size, worst_ref, lengths_ref, place_ref, q_hbm, k_hbm, v_hbm, window_hbm, given, out_hbm,
+def repair(worst_ref, lengths_ref, q_hbm, k_hbm, v_hbm, window_hbm, given, out_hbm,
            queries, block_rows, values_t, marks, result, top, acc, pass_sem):
     @pl.when(worst_ref[0, 0] <= 0.0)
     def _():
@@ -275,8 +275,9 @@
 
     @pl.when(worst_ref[0, 0] > 0.0)
     def _():
-        o, c = place_ref[0], place_ref[1]
+        o, c = lax.axis_index("outer"), lax.axis_index("inner")
         here = o * GROUP + c
+        steps = words_for(c * 2 + o % 2, STEPS)
         starts, ends = edges(lengths_ref)
         pltpu.sync_copy(q_hbm, queries)
         marks[...] = jnp.where(inside(here, starts, ends), 1.0, 0.0).astype(jnp.bfloat16)
@@ -309,7 +310,7 @@
 
         def one(step, _):
             pltpu.sync_copy(window_hbm.at[step], block_rows)
-            block = here - place_ref[2 + step]
+            block = block_at(o, c, unpack(steps, step, 4, 6) & 15)
             scan(with_marks(block, block_rows[0:TOK, :], starts, ends), turned(block_rows), False)
             return 0
 
@@ -319,13 +320,6 @@
             result[:, head * HEAD:(head + 1) * HEAD] = (
                 acc[0:HEAD, columns] / acc[HEAD:HEAD + 1, columns]).T.astype(jnp.bfloat16)
         pltpu.sync_copy(result, out_hbm)
-
-
-def distances(kind):
-    c = kind // 2
-    codes = [(STEPS[kind][step // 4] >> (6 * (step % 4))) & 15 for step in range(REACH)]
-    return [8 + c - slot if slot < 8 else (c - slot + 8 if slot - 8 < c else 16 + c - (slot - 8))
-            for slot in codes]
 
 
 def per_device(outers, queries, keys, values, doc_lengths):
@@ -354,13 +348,10 @@
             flops=4 * 12 * QHEADS * TOK * TOK * HEAD, bytes_accessed=12 << 20,
             transcendentals=12 * QHEADS * TOK * TOK),
     )(doc_lengths, queries, keys, values)
-    o, c = lax.axis_index("outer"), lax.axis_index("inner")
-    table = jnp.array([distances(kind) for kind in range(2 * GROUP)], jnp.int32)
-    place = jnp.concatenate([jnp.stack([o, c]).astype(jnp.int32), table[c * 2 + o % 2]])
     return pl.pallas_call(
-        functools.partial(repair, outers),
+        repair,
         out_shape=out_shape,
-        in_specs=[smem, smem, smem] + [anywhere] * 5,
+        in_specs=[smem, smem] + [anywhere] * 5,
         out_specs=anywhere,
         scratch_shapes=[
             pltpu.VMEM((TOK, QHEADS * HEAD), jnp.bfloat16),
@@ -373,7 +364,7 @@
             pltpu.SemaphoreType.DMA((2, 4)),
         ],
         compiler_params=pltpu.CompilerParams(vmem_limit_bytes=56 << 20),
-    )(worst, doc_lengths, place, queries, keys, values, window, first)
+    )(worst, doc_lengths, queries, keys, values, window, first)
 
 
 def solution(mesh):

time: 85.8 us -> 84.5 us (0.985)
  no operation moved by 1% of the time
where the time goes in v3:
time: 84.5 us; the launch traced here: 84.2 us
  Pallas kernels  84 us (99%)
    pallas_call x1, Pallas kernels, per_device(): pl.pallas_call(functools.partial(kernel, outers), out_shape=(out_shape, j...  81.3 us
    pallas_call x1, Pallas kernels, per_device(): pl.pallas_call(repair, out_shape=out_shape, in_specs=[smem, smem] + [anyw...  2.72 us

profile of v3, /device:TPU:40, one launch (start us, length us, event | category | flops | bytes accessed | tf_op | source)
XLA Modules:
  0.0 84.2 jit_solution(8811352228495553863)
XLA Ops:
  0.0 81.3 %shard_map.46 = (bf16[1024,512]{1,0:T(8,128)(2,1)}, f32[8,128]{1,0:T(8,128)}, bf16[11,2048,128]{2,1,0:T(8,128)(2,1)}) custom-call(s32[16]{0:T(128)} %lengths_ref.3, bf16[1024,512]{1,0:T(8,128)(2,1)} %q_hbm.1, bf16[1024,128]{1,0:T(8,128)(2,1)} %k_hbm.1, bf16[1024,128]{1,0:T(8,128)(2,1)} %v_hbm.1), custom_call_target="tpu_custom_call" | custom-call | flops 25769803776 | bytes 12582912 | tf_op jit(solution)/shard_map/pallas_call | solution.py:330
  81.3 2.7 %shard_map.47 = bf16[1024,512]{1,0:T(8,128)(2,1)} custom-call(f32[8,128]{1,0:T(8,128)} %get-tuple-element.8.worst_ref, s32[16]{0:T(128)} %lengths_ref.3, bf16[1024,512]{1,0:T(8,128)(2,1)} %q_hbm.1, bf16[1024,128]{1,0:T(8,128)(2,1)} %k_hbm.1, bf16[1024,128]{1,0:T(8,128)(2,1)} %v_hbm.1, bf16[11,2048,128]{2,1,0:T(8,128)(2,1)} %get-tuple-element.9.window_hbm, ...), custom_call_target="tpu_custom_call" | custom-call | tf_op jit(solution)/shard_map/pallas_call | solution.py:351

commit v4 on v3

--- a/solution.py
+++ b/solution.py
@@ -21,58 +21,58 @@
 
 
 SENDS = [
-    [606160960, 304096322, 268512322, 415672322, 339879936, 281485708, 667922566, 667871134, 869150852, 659279509, 0, 0, 0, 0, 0],
-    [840987714, 136342594, 841053248, 136408128, 436218880, 818295810, 440604311, 440538773, 198109712, 198142084, 898429192, 822700694, 193727291, 2873, 0],
-    [610355392, 878733506, 442574016, 272836742, 605103298, 605038724, 411411095, 437280802, 357256985, 931942171, 285781818, 0, 0, 0, 0],
-    [845182146, 979374274, 140534978, 440537121, 974154389, 193849610, 881071897, 952623105, 198175512, 444887437, 98470847, 0, 0, 0, 0],
-    [614549824, 882993472, 344270146, 609396032, 344207757, 609432898, 294466726, 441590552, 290172860, 437379238, 0, 0, 0, 0, 0],
-    [983590210, 849350978, 144733506, 139638024, 898495652, 198108327, 844261774, 902764447, 135303203, 100789148, 100725794, 98470847, 0, 0, 0],
-    [618744256, 887185856, 887120322, 281422220, 613785998, 613730336, 298829858, 298723726, 277213086, 277114780, 10771, 0, 0, 0, 0],
-    [148927938, 148993472, 144029070, 902804876, 907088168, 907048232, 982868894, 444960935, 436302882, 978479633, 105090181, 0, 0, 0, 0],
-    [622938688, 958427714, 320941634, 352858640, 387981840, 357282322, 303112589, 424298663, 609397926, 370177819, 298722206, 23817, 0, 0, 0],
-    [857805376, 153185858, 924870208, 319320726, 840012207, 894137244, 907047707, 113697692, 113749124, 109350155, 0, 0, 0, 0, 0],
-    [627133120, 895513282, 895578816, 424356502, 622404246, 622340756, 428651156, 320351000, 285815579, 784771337, 420033040, 303081738, 613806640, 18729, 0],
-    [157378240, 157312706, 152675988, 898495257, 323708071, 143977240, 911369248, 911412623, 3469, 0, 0, 0, 0, 0, 0],
-    [631327552, 899707714, 899773248, 329263896, 294466328, 361581237, 290075418, 348598932, 626730281, 962284081, 957958707, 11562, 0, 0, 0],
-    [161507138, 161572672, 156935962, 915731357, 915771823, 152625813, 902787732, 920086198, 844326580, 113675663, 0, 0, 0, 0, 0],
-    [635521984, 836856768, 903967680, 971072448, 298791838, 622441372, 630999866, 298725905, 622375442, 957948699, 819342236, 424323998, 966615470, 886530347, 962259372],
-    [165680066, 852979119, 152694189, 924324664, 924411308, 122334739, 848629399, 0, 0, 0, 0, 0, 0, 0, 0],
+    [606160960, 304100416, 438380546, 335552514, 281424268, 285815049, 667918734, 667824262, 352921533, 663595536, 0, 0, 0, 0],
+    [136408128, 975266880, 136342594, 975201346, 302066690, 872428940, 189437853, 889743492, 198144398, 894132752, 189467319, 94145204, 13579, 0],
+    [610355392, 878799040, 339879106, 442572932, 605037760, 605104393, 927705222, 290136064, 927642656, 806367629, 396111674, 0, 0, 0],
+    [140534978, 845182146, 979374274, 135312516, 974154389, 827027722, 193763099, 881094920, 198173728, 898462092, 98492947, 98536251, 2873, 0],
+    [614549824, 882993472, 344208706, 609461570, 415672586, 294504612, 441590552, 290170022, 931950362, 0, 0, 0, 0, 0],
+    [144733506, 983590208, 849416514, 139699464, 898397350, 844313864, 885482661, 902797213, 978456611, 198142348, 98560924, 98496910, 100790668, 3073],
+    [618744256, 820013506, 820079040, 281425346, 281487756, 613697571, 348604714, 936321950, 445915403, 873557916, 294499626, 18599, 0, 0],
+    [987828672, 987763138, 982880553, 144010142, 907113505, 449209246, 139703299, 814025729, 139594885, 831304836, 982805009, 0, 0, 0],
+    [622938688, 958493248, 419964482, 420028944, 357278621, 432949677, 303115296, 780465945, 613796137, 0, 0, 0, 0, 0],
+    [857805376, 153185856, 924935744, 907128336, 319320988, 961228306, 894046639, 835588261, 911348011, 839978119, 373493134, 105046414, 0, 0],
+    [627133120, 962620098, 962685632, 357246658, 290140822, 622438080, 361540244, 424288786, 285755953, 419981478, 1003398310, 1003481252, 303160717, 0],
+    [157378240, 157312706, 965546547, 144043173, 143979027, 109438514, 109374234, 839969958, 113741197, 0, 0, 0, 0, 0],
+    [631327552, 899773248, 899707714, 428616472, 294463298, 428690103, 424288916, 361581237, 365949620, 348598803, 12817, 0, 0, 0],
+    [866194240, 866128706, 156935960, 915796892, 915706287, 844360606, 861627031, 920063505, 113741331, 3469, 0, 0, 0, 0],
+    [635521984, 971074496, 903963586, 836793280, 432939932, 630993822, 631065137, 966536094, 365840947, 890774299, 298802837, 311749170, 370193044, 0],
+    [165745600, 920097329, 920020398, 852890163, 161279536, 965600555, 956949273, 961154709, 907087511, 0, 0, 0, 0, 0],
 ]
 COUNTS = [
-    [794754, 2921032, 4518732, 5326034, 5326100, 5326100],
-    [2654728, 2929354, 4522892, 5850322, 7190168, 7190235],
-    [1589508, 3723977, 4785168, 5858578, 5858710, 5858710],
-    [1597830, 2658887, 3990283, 5321809, 5858645, 5858710],
-    [1327364, 2925127, 4522893, 5326098, 5326100, 5326100],
-    [1859974, 3453576, 4527054, 6116627, 6391319, 6391320],
-    [1597830, 3723977, 5055503, 5592340, 5592405, 5592405],
-    [1327364, 2920966, 4260749, 5317713, 5854549, 5858710],
-    [1589508, 3195594, 4522893, 6124883, 6125015, 6125015],
-    [1597830, 2392582, 3723978, 4522958, 5325970, 5326100],
-    [1597830, 3723977, 5584016, 6657558, 7190234, 7190235],
-    [1327364, 2396678, 3195659, 3728268, 4527184, 4527185],
-    [1597830, 3990282, 5317712, 6125014, 6125015, 6125015],
-    [1327364, 2392583, 3457674, 4523022, 5059730, 5326100],
-    [2130440, 4518731, 6382867, 7989018, 7989150, 7989150],
-    [532610, 2388356, 2929290, 3461963, 3728269, 3728270],
+    [1056898, 3187336, 4256653, 5326034, 5326100, 5326100],
+    [2392584, 2929289, 4518732, 6382866, 6657625, 6657625],
+    [1327364, 3461833, 5055567, 5592339, 5858710, 5858710],
+    [1859974, 2662984, 3994444, 5317711, 6387093, 6657625],
+    [1327364, 2662983, 3990348, 4793423, 4793490, 4793490],
+    [1859974, 3195528, 4789198, 6649172, 7190169, 7190235],
+    [1859974, 3990282, 5584017, 6124950, 6125015, 6125015],
+    [1065220, 2920901, 3728140, 5317776, 5858710, 5858710],
+    [1327364, 2662919, 4260684, 4523024, 4793490, 4793490],
+    [1859974, 2929223, 4256588, 5850257, 6391319, 6391320],
+    [1859974, 4256587, 5850322, 6923799, 6923930, 6923930],
+    [1065220, 1864133, 2925063, 4252557, 4789264, 4793490],
+    [1597830, 3728138, 5321808, 5592405, 5592405, 5592405],
+    [1327364, 2654726, 3457739, 4252557, 5055632, 5059795],
+    [2130440, 4256587, 5850258, 6919767, 6923930, 6923930],
+    [532610, 2388356, 3461835, 4785166, 4793490, 4793490],
 ]
 STEPS = [
-    [13834480, 13128189, 257471],
-    [13843568, 10168773, 250815],
-    [5705265, 13397906, 227647],
-    [9906737, 6043654, 214014],
-    [14326898, 12727679, 216536],
-    [5807346, 201223, 214005],
-    [6073907, 12930066, 236918],
-    [6260403, 9542674, 217206],
-    [9264692, 12883383, 241378],
-    [6520180, 988571, 241218],
-    [13868853, 10631302, 225979],
-    [6580021, 14593588, 205051],
-    [12008822, 15156010, 245303],
-    [2808310, 9883227, 15924],
-    [15617975, 6968716, 237101],
-    [3002295, 1549622, 237432],
+    [13061360, 14088343, 257878],
+    [13835504, 16636263, 191890],
+    [9113137, 13778821, 224767],
+    [10640561, 5454854, 58327],
+    [5872754, 16604195, 232759],
+    [2571698, 4152391, 213016],
+    [4947635, 12936752, 216409],
+    [2788851, 9963122, 138596],
+    [13458996, 10426534, 44651],
+    [6512116, 7040219, 207425],
+    [3382581, 2075814, 243928],
+    [7511477, 14427402, 241896],
+    [3648886, 15036723, 245308],
+    [2809334, 15832411, 15876],
+    [3362743, 10641110, 237418],
+    [12109559, 1393080, 110205],
 ]
 OWN = 16
 PARTS = 17

time: 84.5 us -> 92 us (1.089)
  Pallas kernels: 84 us -> 91.6 us
    pallas_call x1, Pallas kernels: 81.3 us -> 88.9 us  [per_device(): pl.pallas_call(functools.partial(kernel, outers), out_shape=(out_shape, j...]
where the time goes in v4:
time: 92 us; the launch traced here: 91.8 us
  Pallas kernels  91.6 us (100%)
    pallas_call x1, Pallas kernels, per_device(): pl.pallas_call(functools.partial(kernel, outers), out_shape=(out_shape, j...  88.9 us
    pallas_call x1, Pallas kernels, per_device(): pl.pallas_call(repair, out_shape=out_shape, in_specs=[smem, smem] + [anyw...  2.72 us

profile of v4, /device:TPU:40, one launch (start us, length us, event | category | flops | bytes accessed | tf_op | source)
XLA Modules:
  0.0 91.8 jit_solution(17438757798709560106)
XLA Ops:
  0.0 88.9 %shard_map.46 = (bf16[1024,512]{1,0:T(8,128)(2,1)}, f32[8,128]{1,0:T(8,128)}, bf16[11,2048,128]{2,1,0:T(8,128)(2,1)}) custom-call(s32[16]{0:T(128)} %lengths_ref.3, bf16[1024,512]{1,0:T(8,128)(2,1)} %q_hbm.1, bf16[1024,128]{1,0:T(8,128)(2,1)} %k_hbm.1, bf16[1024,128]{1,0:T(8,128)(2,1)} %v_hbm.1), custom_call_target="tpu_custom_call" | custom-call | flops 25769803776 | bytes 12582912 | tf_op jit(solution)/shard_map/pallas_call | solution.py:330
  88.9 2.7 %shard_map.47 = bf16[1024,512]{1,0:T(8,128)(2,1)} custom-call(f32[8,128]{1,0:T(8,128)} %get-tuple-element.8.worst_ref, s32[16]{0:T(128)} %lengths_ref.3, bf16[1024,512]{1,0:T(8,128)(2,1)} %q_hbm.1, bf16[1024,128]{1,0:T(8,128)(2,1)} %k_hbm.1, bf16[1024,128]{1,0:T(8,128)(2,1)} %v_hbm.1, bf16[11,2048,128]{2,1,0:T(8,128)(2,1)} %get-tuple-element.9.window_hbm, ...), custom_call_target="tpu_custom_call" | custom-call | tf_op jit(solution)/shard_map/pallas_call | solution.py:351
